TPU v7x, 256 devices: a whole 4x4x8 slice. The times are simulated.
256 devices in a mesh: row: 16 (over x_lo, y, core), line: 16 (over z, x_hi).
Axes of the slice: x: 4 (x_hi: 2, x_lo: 2; x = x_hi * 2 + x_lo), y: 4, z: 8, core: 2. Of those that a mesh axis runs over, the one named last changes fastest.
Arguments:
- scalar: float32 [16, 768, 3072], P('line', 'row'), may hold values from -6 to 6
- x_velocity: float32 [6, 192, 768], P(None, 'row', 'line'), may hold values from -1 to 1
- y_velocity: float32 [6, 192, 768], P(None, 'row', 'line'), may hold values from -1 to 1
Outputs:
- remeshed: float32 [16, 768, 3072], P('line', 'row')
All inputs are finite; a program needn't handle non-finite values.
Results may differ from a plain program's by a relative error of at most 0.0003.
Values sent between devices are 32-bit elements; how exact they have to be, the bound alone decides.
No kernel may reach another device: no remote copies, remote signals or barrier semaphores. Data moves between devices by JAX's collectives and lax.ppermute only.
A program may use at most 128 MiB of HBM per device.

v0:
```python
import jax
import jax.numpy as jnp
from jax import lax
from jax.sharding import PartitionSpec as P

TIME_STEP = 1.6


def padded(cells, sides, width):
    for axis, dim in sides:
        count = lax.axis_size(axis)
        head = lax.slice_in_dim(cells, 0, width, axis=dim)
        tail = lax.slice_in_dim(cells, cells.shape[dim] - width, cells.shape[dim], axis=dim)
        cells = jnp.concatenate(
            [
                lax.ppermute(tail, axis, [(i, (i + 1) % count) for i in range(count)]),
                cells,
                lax.ppermute(head, axis, [((i + 1) % count, i) for i in range(count)]),
            ],
            axis=dim,
        )
    return cells


def tent_weight(values):
    return jnp.maximum(0.0, 1.0 - jnp.abs(values))


def kernel_m6(values):
    radius = jnp.abs(values)
    inside = (
        -(radius - 1.0)
        * (25.0 * radius**4 - 38.0 * radius**3 - 3.0 * radius**2 + 12.0 * radius + 12.0)
        / 12.0
    )
    middle = (
        (radius - 1.0)
        * (radius - 2.0)
        * (25.0 * radius**3 - 114.0 * radius**2 + 153.0 * radius - 48.0)
        / 24.0
    )
    outside = -(radius - 2.0) * (radius - 3.0) ** 3 * (5.0 * radius - 8.0) / 24.0
    return jnp.where(
        radius < 1.0, inside, jnp.where(radius < 2.0, middle, jnp.where(radius < 3.0, outside, 0.0))
    )


def wrap_pad(values, along):
    length_axis = values.shape[along]
    low_side = lax.slice_in_dim(values, length_axis - 3, length_axis, axis=along)
    high_side = lax.slice_in_dim(values, 0, 3, axis=along)
    return jnp.concatenate([low_side, values, high_side], axis=along)


def line_velocity(coarse, displacement, offset, lead_rows, along):
    row_count = displacement.shape[along]
    refined = jnp.repeat(coarse, 4, axis=along)
    shape_list = [1] * displacement.ndim
    shape_list[along] = row_count
    phases = ((jnp.arange(row_count) - lead_rows) % 4).astype(jnp.float32).reshape(shape_list)
    summed = jnp.zeros(displacement.shape, jnp.float32)
    for spread in (-1, 0, 1):
        begin_at = offset + 4 * spread
        picked = lax.slice_in_dim(refined, begin_at, begin_at + row_count, axis=along)
        summed = summed + picked * tent_weight((phases - 1.5 + displacement) / 4.0 - spread)
    return summed


def heun_shift(values, coarse, offset, lead_rows, along):
    resting = line_velocity(coarse, jnp.zeros(values.shape, jnp.float32), offset, lead_rows, along)
    moving = line_velocity(coarse, TIME_STEP * resting, offset, lead_rows, along)
    return 0.5 * TIME_STEP * (resting + moving)


def remesh_periodic(values, displacement, along):
    summed = jnp.zeros(values.shape, jnp.float32)
    for target in range(-4, 5):
        summed = summed + jnp.roll(values * kernel_m6(target - displacement), target, axis=along)
    return summed


def z_weights(planes, coarse_planes):
    fine_index = jnp.arange(planes).astype(jnp.float32)[:, None]
    coarse_index = jnp.arange(coarse_planes).astype(jnp.float32)[None, :]
    return tent_weight((fine_index - 1.5) / 4.0 + 1.0 - coarse_index)


def local(scalar, x_velocity, y_velocity):
    planes, row_count, line_length = scalar.shape
    coarse_planes = x_velocity.shape[0]
    all_weights = z_weights(planes * lax.axis_size("line"), coarse_planes)
    plane_weights = lax.dynamic_slice_in_dim(
        all_weights, lax.axis_index("line") * planes, planes, 0
    )
    whole_x, whole_y = (
        lax.all_gather(x_velocity, "line", axis=2, tiled=True),
        lax.all_gather(y_velocity, "line", axis=2, tiled=True),
    )
    x_rim = padded(whole_x, (("row", 1),), 1)
    flat_y = line_velocity(
        x_rim, jnp.zeros((coarse_planes, row_count, whole_x.shape[2]), jnp.float32), 4, 0, 1
    )
    x_lines = jnp.einsum("kq,qyc->kyc", plane_weights, flat_y, precision=lax.Precision.HIGHEST)
    displacement = heun_shift(scalar, wrap_pad(x_lines, 2), 12, 0, 2)
    moved = remesh_periodic(scalar, displacement, 2)
    flat_x = line_velocity(
        wrap_pad(whole_y, 2),
        jnp.zeros((coarse_planes, whole_y.shape[1], line_length), jnp.float32),
        12,
        0,
        2,
    )
    y_lines = jnp.einsum("kq,qcx->kcx", plane_weights, flat_x, precision=lax.Precision.HIGHEST)
    turned = jnp.swapaxes(moved, 1, 2)
    turned_lines = jnp.swapaxes(y_lines, 1, 2)
    columns, column_lines = (
        lax.all_to_all(turned, "row", split_axis=1, concat_axis=2, tiled=True),
        lax.all_to_all(turned_lines, "row", split_axis=1, concat_axis=2, tiled=True),
    )
    displacement = heun_shift(columns, wrap_pad(column_lines, 2), 12, 0, 2)
    columns = remesh_periodic(columns, displacement, 2)
    returned = lax.all_to_all(columns, "row", split_axis=2, concat_axis=1, tiled=True)
    result = jnp.swapaxes(returned, 1, 2)
    return result


def solution(mesh):
    in_specs = (P("line", "row", None), P(None, "row", "line"), P(None, "row", "line"))
    out_specs = P("line", "row", None)
    return jax.shard_map(local, mesh=mesh, in_specs=in_specs, out_specs=out_specs, check_vma=False)
```

profile of v0, /device:TPU:36, one launch (start us, length us, event | category | flops | bytes accessed | tf_op | source)
XLA Modules:
  0.0 344.3 jit_solution(15629344423565458450)
XLA Ops:
  0.0 0.9 copy.220
  0.9 88.3 %all_gather.6 = f32[6,12,768]{1,0,2:T(8,128)S(1)} all-gather(f32[6,12,48]{1,0,2:T(8,128)S(1)} %copy.220), channel_id=1, replica_groups=mesh['row'=16,'line'=16] {'line'}, dimensions={2}, use_global_device_ids=true | all-gather | bytes 235008 | tf_op jit(solution)/shard_map/all_gather | solution.py:96
  89.2 3.6 %fusion.164 = (f32[6,1,768]{1,0,2:T(8,128)}, f32[6,1,768]{1,0,2:T(8,128)}) fusion(f32[6,12,768]{1,0,2:T(8,128)S(1)} %all_gather.6), kind=kLoop, calls=%fused_computation.270 | loop fusion | bytes 73728 | tf_op jit(solution)/shard_map/slice | solution.py:13
  92.9 2.2 copy.221
  95.1 0.1 collective-permute-start
  95.2 2.9 copy.222
  98.1 3.8 %collective-permute-start.1 = (f32[6,1,768]{2,1,0:T(1,128)}, f32[6,1,768]{2,1,0:T(1,128)S(1)}, u32[]{:S(2)}, u32[]{:S(2)}) collective-permute-start(f32[6,1,768]{2,1,0:T(1,128)} %copy.222), channel_id=1, source_target_pairs={{16,0},{32,16},{48,32},{64,48},{80,64},{96,80},{112,96},{128,112},... | collective-permute-start | bytes 55304 | tf_op jit(solution)/shard_map/ppermute | solution.py:18
  101.9 0.1 copy.230
  102.1 83.4 %all_gather.7 = f32[6,12,768]{1,0,2:T(8,128)S(1)} all-gather(f32[6,12,48]{1,0,2:T(8,128)S(1)} %copy.230), channel_id=1, replica_groups=mesh['row'=16,'line'=16] {'line'}, dimensions={2}, use_global_device_ids=true | all-gather | bytes 235008 | tf_op jit(solution)/shard_map/all_gather | solution.py:97
  185.5 0.4 pad_maximum_fusion
  185.9 1.8 copy.231
  187.8 7.0 %broadcast_in_dim.43 = f32[6,12,774,4]{1,3,2,0:T(4,128)} broadcast(f32[6,12,774]{1,2,0:T(8,128)} %copy.231), dimensions={0,1,2} | broadcast | bytes 1114560 | tf_op jit(solution)/shard_map/broadcast_in_dim | solution.py:57
  194.8 14.0 %fusion = f32[6,12,3072]{1,2,0:T(8,128)} fusion(f32[6,12,3096]{1,2,0:T(8,128)} %bitcast.59, f32[3072]{0:T(1024)S(1)} %get-tuple-element.37, f32[3072]{0:T(1024)S(1)} %get-tuple-element.38, f32[3072]{0:T(1024)S(1)} %get-tuple-element.39), kind=kLoop, calls=%fused_computation.1 | loop fusion | flops 1105920 | bytes 3575808 | tf_op jit(solution)/shard_map/add | solution.py:65
  208.8 7.1 %copy.241 = f32[6,12,3072]{2,0,1:T(8,128)} copy(f32[6,12,3072]{1,2,0:T(8,128)} %fusion) | data formatting | bytes 1769472 | tf_op jit(solution)/shard_map/add | solution.py:65
  216.0 0.2 dynamic-slice_reduce_fusion
  216.2 2.3 fusion.160
  218.6 2.8 copy.232
  221.4 0.5 broadcast.1086
  221.9 15.8 %reduce.4 = f32[3072,12]{1,0:T(8,128)} reduce(f32[3072,1,12]{2,1,0:T(1,128)} %bitcast.63, f32[]{:T(128)} %broadcast.1086), dimensions={1}, to_apply=%bitcast.46.reduce_sub_computation | reduce | bytes 294916
  237.7 3.5 %reshape.383 = f32[16,1,2304]{2,1,0:T(1,128)} reshape(f32[3072,12]{1,0:T(8,128)} %reduce.4) | data formatting | bytes 294912
  241.2 8.6 %all-to-all-start.1 = ((f32[16,1,2304]{2,1,0:T(1,128)}), f32[16,1,2304]{2,1,0:T(1,128)}, u32[]{:S(2)}, u32[]{:S(2)}) async-start(f32[16,1,2304]{2,1,0:T(1,128)} %reshape.383), calls=%async_computation.1 | async-start | bytes 294912 | tf_op jit(solution)/shard_map/all_to_all | solution.py:118
  249.9 0.6 subtract_maximum_fusion.7
  250.5 0.5 subtract_maximum_fusion.9
  251.0 1.0 copy.223
  252.1 0.2 broadcast_in_dim.40
  252.3 0.4 reshape.372
  252.7 0.3 fusion.4
  253.0 1.6 fusion.2
  254.6 0.1 maximum_bitcast_fusion
  254.8 0.2 copy.224
  254.9 0.3 broadcast_in_dim.41
  255.2 1.4 fusion.165
  256.6 2.7 copy.246
  259.3 1.3 copy.247
  260.6 0.4 copy.248
  261.0 2.8 fusion.144
  263.8 5.8 %fusion.137 = (f32[1,48,3072]{2,1,0:T(8,128)S(1)}, f32[1,48,3072]{2,1,0:T(8,128)S(1)}, f32[1,48,3072]{2,1,0:T(8,128)S(1)}, f32[1,48,3072]{2,1,0:T(8,128)S(1)}, f...) fusion(f32[1,48,3072]{2,1,0:T(8,128)S(1)} %copy-done, ...), kind=kLoop, calls=%fused_computation.191 | loop fusion | flops 44384256 | bytes 5308416 | tf_op jit(solution)/shard_map/mul | solution.py:78
  269.6 0.2 slice.256
  269.8 0.2 slice.258
  270.0 0.2 slice.260
  270.3 0.2 slice.262
  270.8 1.1 fusion.116
  271.9 1.7 copy.228
  273.6 13.6 %reduce.2 = f32[3072,48]{1,0:T(8,128)S(1)} reduce(f32[3072,1,48]{2,1,0:T(1,128)S(1)} %bitcast.64, f32[]{:T(128)} %broadcast.1086), dimensions={1}, to_apply=%bitcast.44.reduce_sub_computation | reduce | bytes 1179652
  287.2 2.4 reshape.381
  289.6 6.0 %all-to-all-start = ((f32[16,1,9216]{2,1,0:T(1,128)}), f32[16,1,9216]{2,1,0:T(1,128)S(1)}, u32[]{:S(2)}, u32[]{:S(2)}) async-start(f32[16,1,9216]{2,1,0:T(1,128)} %reshape.381), calls=%async_computation | async-start | bytes 1179648 | tf_op jit(solution)/shard_map/all_to_all | solution.py:117
  295.7 1.8 reduce.5
  297.5 2.6 reshape.384
  300.1 0.6 copy.243
  300.7 0.2 copy.234
  300.9 0.2 pad_maximum_fusion.2
  301.1 0.1 broadcast_in_dim.44
  301.3 0.3 broadcast_in_dim.45
  301.6 5.6 %all-to-all-done = f32[16,1,9216]{2,1,0:T(1,128)S(1)} async-done(((f32[16,1,9216]{2,1,0:T(1,128)}), f32[16,1,9216]{2,1,0:T(1,128)S(1)}, u32[]{:S(2)}, u32[]{:S(2)}) %all-to-all-start) | async-done | bytes 589856 | tf_op jit(solution)/shard_map/all_to_all | solution.py:117
  307.2 1.9 reduce.3
  309.2 3.4 reshape.382
  312.6 0.6 copy.229
  313.1 2.1 fusion.73
  315.2 7.7 %fusion.66 = (f32[1,192,768]{1,2,0:T(8,128)S(1)}, f32[1,192,768]{1,2,0:T(8,128)S(1)}, f32[1,192,768]{1,2,0:T(8,128)S(1)}, f32[1,192,768]{1,2,0:T(8,128)S(1)}, f3...) fusion(f32[1,16,192,48]{2,3,1,0:T(8,128)S(1)} %copy.229, ...), kind=kLoop, calls=%fused_computation.91 | loop fusion | flops 44384256 | bytes 5308416 | tf_op jit(solution)/shard_map/mul | solution.py:78
  323.3 2.0 fusion.45
  325.3 0.8 copy.237
  326.1 16.3 %all_to_all.54 = f32[1,192,768]{1,0,2:T(1,128)S(1)} all-to-all(f32[1,192,768]{1,0,2:T(1,128)S(1)} %copy.237), channel_id=1, replica_groups=mesh['row'=16,'line'=16] {'row'}, dimensions={2} | all-to-all | bytes 1179648 | tf_op jit(solution)/shard_map/all_to_all | solution.py:122
  342.4 0.5 copy.238
  342.9 1.1 all_to_all.50
  (48 shorter events, 1.0 us)
Async XLA Ops:
  92.9 9.1 %copy-start.1 = (f32[6,12,48]{2,1,0:T(8,128)S(1)}, f32[6,12,48]{2,1,0:T(8,128)}, u32[]{:S(2)}) copy-start(f32[6,12,48]{2,1,0:T(8,128)} %param.5) | copy-start | bytes 41476
  95.1 156.9 %collective-permute-start = (f32[6,1,768]{2,1,0:T(1,128)S(1)}, f32[6,1,768]{2,1,0:T(1,128)S(1)}, u32[]{:S(2)}, u32[]{:S(2)}) collective-permute-start(f32[6,1,768]{2,1,0:T(1,128)S(1)} %copy.221), channel_id=1, source_target_pairs={{0,16},{16,32},{32,48},{48,64},{64,80},{80,96},{96,112},{112,128},... | collective-permute-start | bytes 55304 | tf_op jit(solution)/shard_map/ppermute | solution.py:16
  98.1 154.0 %collective-permute-start.1 = (f32[6,1,768]{2,1,0:T(1,128)}, f32[6,1,768]{2,1,0:T(1,128)S(1)}, u32[]{:S(2)}, u32[]{:S(2)}) collective-permute-start(f32[6,1,768]{2,1,0:T(1,128)} %copy.222), channel_id=1, source_target_pairs={{16,0},{32,16},{48,32},{64,48},{80,64},{96,80},{112,96},{128,112},... | collective-permute-start | bytes 55304 | tf_op jit(solution)/shard_map/ppermute | solution.py:18
  241.2 48.4 %all-to-all-start.1 = ((f32[16,1,2304]{2,1,0:T(1,128)}), f32[16,1,2304]{2,1,0:T(1,128)}, u32[]{:S(2)}, u32[]{:S(2)}) async-start(f32[16,1,2304]{2,1,0:T(1,128)} %reshape.383), calls=%async_computation.1 | async-start | bytes 294912 | tf_op jit(solution)/shard_map/all_to_all | solution.py:118
  252.0 0.7 copy-start.2
  252.0 0.7 copy-start.3
  252.0 0.7 copy-start.4
  260.6 3.2 copy-start
  289.6 17.6 %all-to-all-start = ((f32[16,1,9216]{2,1,0:T(1,128)}), f32[16,1,9216]{2,1,0:T(1,128)S(1)}, u32[]{:S(2)}, u32[]{:S(2)}) async-start(f32[16,1,9216]{2,1,0:T(1,128)} %reshape.381), calls=%async_computation | async-start | bytes 1179648 | tf_op jit(solution)/shard_map/all_to_all | solution.py:117
where the time goes:
time: 348 us; the launch traced here: 344 us
  blocking collectives  188 us (54%)
  other arithmetic  71 us (20%)
  local copies, waits for them, and re-layouts  56.5 us (16%)
  starting transfers between devices  18.6 us (5%)
  waiting for transfers between devices  5.65 us (2%)
  matrix products  3.91 us (1%)
    all_gather x1, blocking collectives, local(): lax.all_gather(x_velocity, 'line', axis=2, tiled=True)  88.3 us
    all_gather x1, blocking collectives, local(): lax.all_gather(y_velocity, 'line', axis=2, tiled=True)  83.4 us
    unnamed x2, other arithmetic  29.4 us
    mul x4, other arithmetic, remesh_periodic(): values * kernel_m6(target - displacement)  18.3 us
    unnamed x21, local copies, waits for them, and re-layouts  17.9 us
    all_to_all x1, blocking collectives, local(): lax.all_to_all(columns, 'row', split_axis=2, concat_axis=1, tiled=True)  16.3 us
    add x2, other arithmetic, line_velocity(): summed + picked * tent_weight((phases - 1.5 + displacement) / 4.0 - spread)  14.3 us
    all_to_all x1, starting transfers between devices, local(): lax.all_to_all(turned_lines, 'row', split_axis=1, concat_axis=2, tiled=True)  8.64 us
  transfers between devices with their start and end apart: 4, of which 1 were waited for; matrix products, arithmetic and copies ran while one was open for 30% of the time, Pallas kernels for 0%

commit v1 on v0

v1 whole, which is shorter than its diff:
```python
import functools

import jax
import jax.numpy as jnp
import numpy as np
from jax import lax
from jax.experimental import pallas as pl
from jax.experimental.pallas import tpu as pltpu
from jax.sharding import PartitionSpec as P

SEGMENTS, LANES, TILE = 24, 128, 8
GROUP = SEGMENTS * TILE
WINDOW = 64


def kernel_parts():
    a = np.polynomial.Polynomial([0.0, 1.0])
    pieces = (
        -(a - 1) * (25 * a**4 - 38 * a**3 - 3 * a**2 + 12 * a + 12) / 12,
        (a - 1) * (a - 2) * (25 * a**3 - 114 * a**2 + 153 * a - 48) / 24,
        -(a - 2) * (a - 3) ** 3 * (5 * a - 8) / 24,
    )
    parts = []
    for middle, piece in zip((0.5, 1.5, 2.5), pieces):
        coefs = piece(middle - a).coef
        parts.append(([float(c) for c in coefs[0::2]], [float(c) for c in coefs[1::2]]))
    return parts


PARTS = kernel_parts()


def products(value, d):
    high = d >= 0.0
    e = d - jnp.where(high, 1.0, -1.0)
    right = e >= 0.0
    t = jnp.abs(e) - 0.5
    tau = t * t
    vt = value * t
    near, far = [], []
    for even, odd in PARTS:
        ev = value * ((even[2] * tau + even[1]) * tau + even[0])
        od = vt * ((odd[2] * tau + odd[1]) * tau + odd[0])
        near.append(ev + od)
        far.append(ev - od)
    q = {0: far[0]}
    q[1] = jnp.where(right, near[0], far[1])
    q[-1] = jnp.where(right, far[1], near[0])
    q[2] = jnp.where(right, near[1], far[2])
    q[-2] = jnp.where(right, far[2], near[1])
    q[3] = jnp.where(right, near[2], 0.0)
    q[-3] = jnp.where(right, 0.0, near[2])
    out = []
    for s in range(-4, 5):
        up, down = q.get(s - 1), q.get(s + 1)
        out.append(jnp.where(high, 0.0 if up is None else up, 0.0 if down is None else down))
    return out


def interp_matrices():
    half = np.zeros((128, 256))
    ident = np.zeros((128, 256))
    plus = np.zeros((128, 256))
    minus = np.zeros((128, 256))
    for fine in range(256):
        c, v = fine // 4 + 32, (fine % 4 - 1.5) / 4
        half[c, fine] += 0.5 * (1 - abs(v))
        half[c + (1 if v > 0 else -1), fine] += 0.5 * abs(v)
        ident[c, fine] = 1
        plus[c + 1, fine], plus[c, fine] = 1, -1
        minus[c, fine], minus[c - 1, fine] = 1, -1
    full = np.concatenate([half, 2 * half + ident, plus, minus], axis=1)
    both = np.concatenate([full, full], axis=0)
    both[0, :256] = (np.arange(256) % 4 - 1.5) / 4
    both[128, :256] = 0
    return both


def row_matrix():
    a = np.zeros((64, 16))
    for row in range(4, 60):
        y = row - 8
        c, v = y // 4 + 2, (y % 4 - 1.5) / 4
        a[row, c] += 1 - abs(v)
        a[row, c + (1 if v > 0 else -1)] += abs(v)
    return np.concatenate([a, a], axis=1)


def z_pair(k):
    at = (k - 1.5) / 4 + 1
    q = int(np.floor(at))
    return q, at - q


def pack_kernel(x_ref, y_ref, out_ref, both):
    both[...] = jnp.zeros_like(both)
    both[:, :, 0:48] = x_ref[...]
    both[:, :, 64:112] = y_ref[...]
    for k in range(16):
        q, w = z_pair(k)
        out_ref[k] = (1 - w) * both[q] + w * both[q + 1]


def pack(x, y):
    return pl.pallas_call(
        pack_kernel,
        out_shape=jax.ShapeDtypeStruct((16, 16, 128), jnp.float32),
        scratch_shapes=[pltpu.VMEM((6, 16, 128), jnp.float32)],
        name="pack_planes",
    )(x, y)


def split(values):
    high = values.astype(jnp.bfloat16)
    low = (values - high.astype(jnp.float32)).astype(jnp.bfloat16)
    return high, low


def windows(lines, left, first):
    rows = lines.shape[0]
    lane0 = lax.broadcasted_iota(jnp.int32, (rows, 128), 1) == 0
    for m in range(12):
        shift = 32 if m % 2 == 0 else 96
        if m < 2:
            rolled = pltpu.roll(lines, shift, 1)
            if m == 0:
                even = rolled
            else:
                odd = rolled
        source = even if m % 2 == 0 else odd
        at = (64 * m - 32 + shift) % 768
        part = jnp.where(lane0, first, source[:, at : at + 128])
        high, low = split(part)
        left[m * rows : (m + 1) * rows, 0:128] = high
        left[m * rows : (m + 1) * rows, 128:256] = low


def row_start(row):
    return (row // TILE) * GROUP + row % TILE


def sweep_kernel(got, scalar, top, bottom, matrix, rows_matrix, out, gx, gy, left_x, left_y, coefs, ylines, source, moved):
    for j in range(16):
        gx[:, 48 * j : 48 * j + 48] = got[j, :, 0:48]
        gy[:, 48 * j : 48 * j + 48] = got[j, :, 64:112]
    high, low = split(gx[...])
    lines = jnp.dot(rows_matrix[...], jnp.concatenate([high, low], axis=0), preferred_element_type=jnp.float32)
    windows(0.8 * lines, left_x, 1.0)
    windows(1.6 * gy[...], left_y, 0.0)
    for q in range(4):
        res = jnp.dot(left_x[...], matrix[:, 256 * q : 256 * q + 256], preferred_element_type=jnp.float32)
        for m in range(12):
            for h in range(2):
                for t in range(8):
                    at = (t * SEGMENTS + 2 * m + h) * TILE
                    coefs[q, at : at + TILE, :] = res[m * 64 + 8 * t : m * 64 + 8 * t + 8, 128 * h : 128 * h + 128]
    res = jnp.dot(left_y[...], matrix[:, 0:256], preferred_element_type=jnp.float32)
    for m in range(12):
        for h in range(2):
            for t in range(2):
                at = (t * SEGMENTS + 2 * m + h) * TILE
                ylines[at : at + TILE, :] = res[m * 16 + 8 * t : m * 16 + 8 * t + 8, 128 * h : 128 * h + 128]
    source[0:GROUP, :] = top[...]
    source[GROUP : 7 * GROUP, :] = scalar[...]
    source[7 * GROUP :, :] = bottom[...]

    lane = lax.broadcasted_iota(jnp.int32, (SEGMENTS, LANES), 1)

    def x_rows(block, carry):
        for r in range(4):
            row = block * 4 + r
            at = pl.ds(row_start(row), SEGMENTS, stride=TILE)
            v, s, dp, dm = (coefs[q, at, :] for q in range(4))
            d = s + v * jnp.where(v >= 0.0, dp, dm)
            parts = products(source[at, :], d)
            total = parts[4]
            ahead = behind = None
            for s in range(1, 5):
                moved_up = pltpu.roll(parts[4 + s], s, 1)
                over = jnp.where(lane < s, moved_up, 0.0)
                ahead = over if ahead is None else ahead + over
                moved_down = pltpu.roll(parts[4 - s], LANES - s, 1)
                under = jnp.where(lane >= LANES - s, moved_down, 0.0)
                behind = under if behind is None else behind + under
                total = total + (moved_up + moved_down)
            total = total - (ahead + behind)
            total = total + (pltpu.roll(ahead, 1, 0) + pltpu.roll(behind, SEGMENTS - 1, 0))
            moved[row] = total
        return carry

    lax.fori_loop(1, 15, x_rows, 0)

    def y_cell(store, cell, carry):
        below, here, above = (ylines[pl.ds(row_start(cell + k), SEGMENTS, stride=TILE), :] for k in (-1, 0, 1))
        dm, dp = here - below, above - here
        acc = list(carry) + [None] * 4
        for r in range(4):
            v0 = (r - 1.5) / 4
            u0 = here + v0 * (dp if v0 > 0 else dm)
            v = v0 + 0.5 * u0
            d = (u0 + here) + v * jnp.where(v >= 0.0, dp, dm)
            parts = products(moved[cell * 4 + r], d)
            for s in range(9):
                acc[r + s] = parts[s] if acc[r + s] is None else acc[r + s] + parts[s]
        if store:
            for r in range(4):
                row = 4 * (cell - 2) + r - 4
                out[pl.ds(row_start(row), SEGMENTS, stride=TILE), :] = acc[r]
        return tuple(acc[4:])

    zero = jnp.zeros((SEGMENTS, LANES), jnp.float32)
    carry = lax.fori_loop(1, 3, functools.partial(y_cell, False), (zero,) * 8)
    lax.fori_loop(3, 15, functools.partial(y_cell, True), carry)


def sweeps(got, scalar, top, bottom):
    matrix = jnp.asarray(interp_matrices(), jnp.bfloat16)
    rows_matrix = jnp.asarray(row_matrix(), jnp.bfloat16)
    return pl.pallas_call(
        sweep_kernel,
        out_shape=jax.ShapeDtypeStruct((6 * GROUP, LANES), jnp.float32),
        scratch_shapes=[
            pltpu.VMEM((16, 768), jnp.float32),
            pltpu.VMEM((16, 768), jnp.float32),
            pltpu.VMEM((12 * 64, 256), jnp.bfloat16),
            pltpu.VMEM((12 * 16, 256), jnp.bfloat16),
            pltpu.VMEM((4, 8 * GROUP, LANES), jnp.float32),
            pltpu.VMEM((2 * GROUP, LANES), jnp.float32),
            pltpu.VMEM((8 * GROUP, LANES), jnp.float32),
            pltpu.VMEM((64, SEGMENTS, LANES), jnp.float32),
        ],
        compiler_params=pltpu.CompilerParams(vmem_limit_bytes=32 * 2**20),
        name="sweeps",
    )(got, scalar, top, bottom, matrix, rows_matrix)


def local(scalar, x_velocity, y_velocity):
    count = lax.axis_size("row")
    up = [(i, (i + 1) % count) for i in range(count)]
    down = [((i + 1) % count, i) for i in range(count)]
    tiles = scalar.reshape(6, TILE, SEGMENTS, LANES).transpose(0, 2, 1, 3).reshape(6 * GROUP, LANES)
    pair = jnp.stack([x_velocity, y_velocity])
    low = lax.ppermute(pair[:, :, 10:], "row", up)
    high = lax.ppermute(pair[:, :, :2], "row", down)
    pair = jnp.concatenate([low, pair, high], axis=2)
    top = lax.ppermute(tiles[5 * GROUP :], "row", up)
    bottom = lax.ppermute(tiles[:GROUP], "row", down)
    got = lax.all_to_all(pack(pair[0], pair[1]), "line", 0, 0, tiled=True)
    result = sweeps(got, tiles, top, bottom)
    return result.reshape(6, SEGMENTS, TILE, LANES).transpose(0, 2, 1, 3).reshape(1, 48, 3072)


def solution(mesh):
    in_specs = (P("line", "row", None), P(None, "row", "line"), P(None, "row", "line"))
    out_specs = P("line", "row", None)
    return jax.shard_map(local, mesh=mesh, in_specs=in_specs, out_specs=out_specs, check_vma=False)
```

time: 348 us -> 38.4 us (0.11)
  the two profiles are of different devices: /device:TPU:36 before, /device:TPU:1 now
where the time goes in v1:
time: 38.4 us; the launch traced here: 37.9 us
  starting transfers between devices  16.3 us (42%)
  waiting for transfers between devices  10.6 us (28%)
  Pallas kernels  8.56 us (22%)
  other arithmetic  1.71 us (4%)
  local copies, waits for them, and re-layouts  0.67 us (2%)
    all_to_all x1, starting transfers between devices, local(): got = lax.all_to_all(pack(pair[0], pair[1]), 'line', 0, 0, tiled=True)  11 us
    pallas_call x1, Pallas kernels, sweeps(): pl.pallas_call(sweep_kernel, out_shape=jax.ShapeDtypeStruct((6 * GROUP, L...  6.99 us
    all_to_all x1, waiting for transfers between devices, local(): got = lax.all_to_all(pack(pair[0], pair[1]), 'line', 0, 0, tiled=True)  5.17 us
    ppermute x1, starting transfers between devices, local(): low = lax.ppermute(pair[:, :, 10:], 'row', up)  2.76 us
    ppermute x1, waiting for transfers between devices, local(): bottom = lax.ppermute(tiles[:GROUP], 'row', down)  2.3 us
    ppermute x1, waiting for transfers between devices, local(): high = lax.ppermute(pair[:, :, :2], 'row', down)  1.89 us
    pallas_call x1, Pallas kernels, pack(): pl.pallas_call(pack_kernel, out_shape=jax.ShapeDtypeStruct((16, 16, 128),...  1.57 us
    ppermute x1, starting transfers between devices, local(): bottom = lax.ppermute(tiles[:GROUP], 'row', down)  1.02 us
  transfers between devices with their start and end apart: 5, of which 5 were waited for; matrix products, arithmetic and copies ran while one was open for 0% of the time, Pallas kernels for 0%

profile of v1, /device:TPU:1, one launch (start us, length us, event | category | flops | bytes accessed | tf_op | source)
XLA Modules:
  0.0 37.9 jit_solution(17551221000958582489)
XLA Ops:
  0.0 0.0 copy-start
  0.0 0.9 %pad_maximum_fusion.2 = (f32[2,6,2,48]{3,2,1,0:T(2,128)S(1)}, f32[2,6,2,48]{3,2,1,0:T(2,128)S(1)}) fusion(f32[1,6,12,48]{3,2,1,0:T(8,128)} %bitcast.22, f32[1,6,12,48]{3,2,1,0:T(8,128)} %bitcast.24), kind=kLoop, calls=%fused_computation.6 | loop fusion | flops 2304 | bytes 36864 | tf_op jit(solution)/shard_map/slice | solution.py:243
  0.9 2.8 %collective-permute-start = (f32[2,6,2,48]{3,2,1,0:T(2,128)S(1)}, f32[2,6,2,48]{3,2,1,0:T(2,128)S(1)}, u32[]{:S(2)}, u32[]{:S(2)}) collective-permute-start(f32[2,6,2,48]{3,2,1,0:T(2,128)S(1)} %get-tuple-element.9), channel_id=1, source_target_pairs={{0,16},{16,32},{32,48},{48,64},{64,80},{80,96},{96,112},{112,128},... | collective-permute-start | bytes 13832 | tf_op jit(solution)/shard_map/ppermute | solution.py:243
  3.6 0.6 %collective-permute-start.1 = (f32[2,6,2,48]{3,2,1,0:T(2,128)S(1)}, f32[2,6,2,48]{3,2,1,0:T(2,128)S(1)}, u32[]{:S(2)}, u32[]{:S(2)}) collective-permute-start(f32[2,6,2,48]{3,2,1,0:T(2,128)S(1)} %get-tuple-element.10), channel_id=1, source_target_pairs={{16,0},{32,16},{48,32},{64,48},{80,64},{96,80},{112,96},{128,112},... | collective-permute-start | bytes 13832 | tf_op jit(solution)/shard_map/ppermute | solution.py:244
  4.3 0.6 %collective-permute-done = f32[2,6,2,48]{3,2,1,0:T(2,128)S(1)} collective-permute-done((f32[2,6,2,48]{3,2,1,0:T(2,128)S(1)}, f32[2,6,2,48]{3,2,1,0:T(2,128)S(1)}, u32[]{:S(2)}, u32[]{:S(2)}) %collective-permute-start) | collective-permute-done | bytes 4640 | tf_op jit(solution)/shard_map/ppermute | solution.py:243
  4.9 1.9 %collective-permute-done.1 = f32[2,6,2,48]{3,2,1,0:T(2,128)S(1)} collective-permute-done((f32[2,6,2,48]{3,2,1,0:T(2,128)S(1)}, f32[2,6,2,48]{3,2,1,0:T(2,128)S(1)}, u32[]{:S(2)}, u32[]{:S(2)}) %collective-permute-start.1) | collective-permute-done | bytes 4640 | tf_op jit(solution)/shard_map/ppermute | solution.py:244
  6.8 0.9 %pad_maximum_fusion = f32[2,6,16,48]{3,2,1,0:T(8,128)S(1)} fusion(f32[2,6,2,48]{3,2,1,0:T(2,128)S(1)} %collective-permute-done.1, f32[1,6,12,48]{3,2,1,0:T(8,128)} %bitcast.23, f32[1,6,12,48]{3,2,1,0:T(8,128)} %bitcast.25, f32[2,6,2,48]{3,2,1,0:T(2,128)S(1)} %collective-permute-done), kind=kLoop, calls=%fused_computation.2 | loop fusion | flops 27648 | bytes 73728 | tf_op jit(solution)/shard_map/concatenate | solution.py:245
  7.6 0.0 copy-start.1
  7.6 0.6 %slice_bitcast_fusion.2 = (f32[6,16,48]{2,1,0:T(8,128)}, f32[6,16,48]{2,1,0:T(8,128)}) fusion(f32[2,6,16,48]{3,2,1,0:T(8,128)S(1)} %pad_maximum_fusion), kind=kLoop, calls=%fused_computation.3 | loop fusion | bytes 73728 | tf_op jit(solution)/shard_map/squeeze | solution.py:248
  8.3 1.6 %pack_planes.1 = f32[16,16,128]{2,1,0:T(8,128)} custom-call(f32[6,16,48]{2,1,0:T(8,128)} %get-tuple-element.8.x_ref, f32[6,16,48]{2,1,0:T(8,128)} %get-tuple-element.7.y_ref), custom_call_target="tpu_custom_call" | custom-call | tf_op jit(solution)/shard_map/pack_planes/pallas_call | solution.py:105
  9.8 11.0 %all-to-all-start = ((f32[16,16,128]{2,1,0:T(8,128)}), f32[16,16,128]{2,1,0:T(8,128)S(1)}, u32[]{:S(2)}, u32[]{:S(2)}) async-start(f32[16,16,128]{2,1,0:T(8,128)} %pack_planes.1), calls=%async_computation | async-start | bytes 262144 | tf_op jit(solution)/shard_map/all_to_all | solution.py:248
  20.9 0.0 copy-done
  20.9 0.0 copy-start.2
  20.9 1.0 %collective-permute-start.3 = (f32[192,128]{1,0:T(8,128)S(1)}, f32[192,128]{1,0:T(8,128)S(1)}, u32[]{:S(2)}, u32[]{:S(2)}) collective-permute-start(f32[192,128]{1,0:T(8,128)S(1)} %get-tuple-element.5), channel_id=1, source_target_pairs={{16,0},{32,16},{48,32},{64,48},{80,64},{96,80},{112,96},{128,112},... | collective-permute-start | bytes 294920 | tf_op jit(solution)/shard_map/ppermute | solution.py:247
  21.9 0.8 %collective-permute-start.2 = (f32[192,128]{1,0:T(8,128)S(1)}, f32[192,128]{1,0:T(8,128)S(1)}, u32[]{:S(2)}, u32[]{:S(2)}) collective-permute-start(f32[192,128]{1,0:T(8,128)S(1)} %get-tuple-element.6), channel_id=1, source_target_pairs={{0,16},{16,32},{32,48},{48,64},{64,80},{80,96},{96,112},{112,128},... | collective-permute-start | bytes 294920 | tf_op jit(solution)/shard_map/ppermute | solution.py:246
  22.8 2.3 %collective-permute-done.3.bottom = f32[192,128]{1,0:T(8,128)S(1)} collective-permute-done((f32[192,128]{1,0:T(8,128)S(1)}, f32[192,128]{1,0:T(8,128)S(1)}, u32[]{:S(2)}, u32[]{:S(2)}) %collective-permute-start.3) | collective-permute-done | bytes 98336 | tf_op jit(solution)/shard_map/ppermute | solution.py:247
  25.0 0.6 %collective-permute-done.2.top = f32[192,128]{1,0:T(8,128)S(1)} collective-permute-done((f32[192,128]{1,0:T(8,128)S(1)}, f32[192,128]{1,0:T(8,128)S(1)}, u32[]{:S(2)}, u32[]{:S(2)}) %collective-permute-start.2) | collective-permute-done | bytes 98336 | tf_op jit(solution)/shard_map/ppermute | solution.py:246
  25.7 5.2 %all-to-all-done.got = f32[16,16,128]{2,1,0:T(8,128)S(1)} async-done(((f32[16,16,128]{2,1,0:T(8,128)}), f32[16,16,128]{2,1,0:T(8,128)S(1)}, u32[]{:S(2)}, u32[]{:S(2)}) %all-to-all-start) | async-done | bytes 131104 | tf_op jit(solution)/shard_map/all_to_all | solution.py:248
  30.9 0.0 copy-done.1
  30.9 0.0 copy-done.2
  30.9 7.0 %sweeps.1 = f32[1152,128]{1,0:T(8,128)} custom-call(f32[16,16,128]{2,1,0:T(8,128)S(1)} %all-to-all-done.got, f32[1152,128]{1,0:T(8,128)S(1)} %bitcast.21, f32[192,128]{1,0:T(8,128)S(1)} %collective-permute-done.2.top, f32[192,128]{1,0:T(8,128)S(1)} %collective-permute-done.3.bottom, bf16[256,1024]{1,0:T(8,128)(2,1)S(1)} %copy-done.1, ...), custom_call_target="tpu_custom_call" | custom-call | tf_op jit(solution)/shard_map/sweeps/pallas_call | solution.py:219
  (1 shorter events, 0.0 us)
Async XLA Ops:
  0.0 20.9 %copy-start = (f32[1,48,3072]{2,1,0:T(8,128)S(1)}, f32[1,48,3072]{2,1,0:T(8,128)}, u32[]{:S(2)}) copy-start(f32[1,48,3072]{2,1,0:T(8,128)} %param.5) | copy-start | bytes 1769476
  0.9 4.0 %collective-permute-start = (f32[2,6,2,48]{3,2,1,0:T(2,128)S(1)}, f32[2,6,2,48]{3,2,1,0:T(2,128)S(1)}, u32[]{:S(2)}, u32[]{:S(2)}) collective-permute-start(f32[2,6,2,48]{3,2,1,0:T(2,128)S(1)} %get-tuple-element.9), channel_id=1, source_target_pairs={{0,16},{16,32},{32,48},{48,64},{64,80},{80,96},{96,112},{112,128},... | collective-permute-start | bytes 13832 | tf_op jit(solution)/shard_map/ppermute | solution.py:243
  3.6 3.1 %collective-permute-start.1 = (f32[2,6,2,48]{3,2,1,0:T(2,128)S(1)}, f32[2,6,2,48]{3,2,1,0:T(2,128)S(1)}, u32[]{:S(2)}, u32[]{:S(2)}) collective-permute-start(f32[2,6,2,48]{3,2,1,0:T(2,128)S(1)} %get-tuple-element.10), channel_id=1, source_target_pairs={{16,0},{32,16},{48,32},{64,48},{80,64},{96,80},{112,96},{128,112},... | collective-permute-start | bytes 13832 | tf_op jit(solution)/shard_map/ppermute | solution.py:244
  7.6 23.2 %copy-start.1 = (bf16[256,1024]{1,0:T(8,128)(2,1)S(1)}, bf16[256,1024]{1,0:T(8,128)(2,1)}, u32[]{:S(2)}) copy-start(bf16[256,1024]{1,0:T(8,128)(2,1)} %constant.4.clone.matrix) | copy-start | bytes 1572868
  9.8 21.0 %all-to-all-start = ((f32[16,16,128]{2,1,0:T(8,128)}), f32[16,16,128]{2,1,0:T(8,128)S(1)}, u32[]{:S(2)}, u32[]{:S(2)}) async-start(f32[16,16,128]{2,1,0:T(8,128)} %pack_planes.1), calls=%async_computation | async-start | bytes 262144 | tf_op jit(solution)/shard_map/all_to_all | solution.py:248
  20.9 10.0 %copy-start.2 = (bf16[64,32]{1,0:T(8,128)(2,1)S(1)}, bf16[64,32]{1,0:T(8,128)(2,1)}, u32[]{:S(2)}) copy-start(bf16[64,32]{1,0:T(8,128)(2,1)} %constant.5.clone.rows_matrix) | copy-start | bytes 12292
  20.9 4.1 %collective-permute-start.3 = (f32[192,128]{1,0:T(8,128)S(1)}, f32[192,128]{1,0:T(8,128)S(1)}, u32[]{:S(2)}, u32[]{:S(2)}) collective-permute-start(f32[192,128]{1,0:T(8,128)S(1)} %get-tuple-element.5), channel_id=1, source_target_pairs={{16,0},{32,16},{48,32},{64,48},{80,64},{96,80},{112,96},{128,112},... | collective-permute-start | bytes 294920 | tf_op jit(solution)/shard_map/ppermute | solution.py:247
  21.9 3.7 %collective-permute-start.2 = (f32[192,128]{1,0:T(8,128)S(1)}, f32[192,128]{1,0:T(8,128)S(1)}, u32[]{:S(2)}, u32[]{:S(2)}) collective-permute-start(f32[192,128]{1,0:T(8,128)S(1)} %get-tuple-element.6), channel_id=1, source_target_pairs={{0,16},{16,32},{32,48},{48,64},{64,80},{80,96},{96,112},{112,128},... | collective-permute-start | bytes 294920 | tf_op jit(solution)/shard_map/ppermute | solution.py:246

commit v2 on v1

v2 whole, which is shorter than its diff:
```python
import functools

import jax
import jax.numpy as jnp
import numpy as np
from jax import lax
from jax.experimental import pallas as pl
from jax.experimental.pallas import tpu as pltpu
from jax.sharding import PartitionSpec as P

SEGMENTS, LANES, TILE = 24, 128, 8
GROUP = SEGMENTS * TILE
WINDOW = 64


def kernel_parts():
    a = np.polynomial.Polynomial([0.0, 1.0])
    pieces = (
        -(a - 1) * (25 * a**4 - 38 * a**3 - 3 * a**2 + 12 * a + 12) / 12,
        (a - 1) * (a - 2) * (25 * a**3 - 114 * a**2 + 153 * a - 48) / 24,
        -(a - 2) * (a - 3) ** 3 * (5 * a - 8) / 24,
    )
    parts = []
    for middle, piece in zip((0.5, 1.5, 2.5), pieces):
        coefs = piece(middle - a).coef
        parts.append(([float(c) for c in coefs[0::2]], [float(c) for c in coefs[1::2]]))
    return parts


PARTS = kernel_parts()


def products(value, d):
    high = d >= 0.0
    e = d - jnp.where(high, 1.0, -1.0)
    right = e >= 0.0
    t = jnp.abs(e) - 0.5
    tau = t * t
    vt = value * t
    near, far = [], []
    for even, odd in PARTS:
        ev = value * ((even[2] * tau + even[1]) * tau + even[0])
        od = vt * ((odd[2] * tau + odd[1]) * tau + odd[0])
        near.append(ev + od)
        far.append(ev - od)
    q = {0: far[0]}
    q[1] = jnp.where(right, near[0], far[1])
    q[-1] = jnp.where(right, far[1], near[0])
    q[2] = jnp.where(right, near[1], far[2])
    q[-2] = jnp.where(right, far[2], near[1])
    q[3] = jnp.where(right, near[2], 0.0)
    q[-3] = jnp.where(right, 0.0, near[2])
    out = []
    for s in range(-4, 5):
        up, down = q.get(s - 1), q.get(s + 1)
        out.append(jnp.where(high, 0.0 if up is None else up, 0.0 if down is None else down))
    return out


def interp_matrices():
    half = np.zeros((128, 256))
    ident = np.zeros((128, 256))
    plus = np.zeros((128, 256))
    minus = np.zeros((128, 256))
    for fine in range(256):
        c, v = fine // 4 + 32, (fine % 4 - 1.5) / 4
        half[c, fine] += 0.5 * (1 - abs(v))
        half[c + (1 if v > 0 else -1), fine] += 0.5 * abs(v)
        ident[c, fine] = 1
        plus[c + 1, fine], plus[c, fine] = 1, -1
        minus[c, fine], minus[c - 1, fine] = 1, -1
    full = np.concatenate([half, 2 * half + ident, plus, minus], axis=1)
    both = np.concatenate([full, full], axis=0)
    both[0, :256] = (np.arange(256) % 4 - 1.5) / 4
    both[128, :256] = 0
    return both


def row_matrix(fine_rows, coarse_rows):
    a = np.zeros((len(fine_rows), len(coarse_rows)))
    for i, y in enumerate(fine_rows):
        c, v = y // 4, (y % 4 - 1.5) / 4
        for cell, weight in ((c, 1 - abs(v)), (c + (1 if v > 0 else -1), abs(v))):
            if cell in coarse_rows:
                a[i, coarse_rows.index(cell)] += weight
    return np.concatenate([a, a], axis=1)


INNER_ROWS, INNER_CELLS = list(range(48)), list(range(16))
EDGE_ROWS = list(range(-4, 4)) + list(range(44, 52))
EDGE_CELLS = [-2, -1, 0, 1, 10, 11, 12, 13]


def z_pair(k):
    at = (k - 1.5) / 4 + 1
    q = int(np.floor(at))
    return q, at - q


def pack_kernel(x_ref, y_ref, out_ref, both):
    both[...] = jnp.zeros_like(both)
    both[:, 0:12, 0:48] = x_ref[...]
    both[:, 0:12, 64:112] = y_ref[...]
    for k in range(16):
        q, w = z_pair(k)
        out_ref[k] = (1 - w) * both[q] + w * both[q + 1]


def pack(x, y):
    return pl.pallas_call(
        pack_kernel,
        out_shape=jax.ShapeDtypeStruct((16, 16, 128), jnp.float32),
        scratch_shapes=[pltpu.VMEM((6, 16, 128), jnp.float32)],
        name="pack_planes",
    )(x, y)


def split(values):
    high = values.astype(jnp.bfloat16)
    low = (values - high.astype(jnp.float32)).astype(jnp.bfloat16)
    return high, low


def windows(lines, left, first):
    rows = lines.shape[0]
    lane0 = lax.broadcasted_iota(jnp.int32, (rows, 128), 1) == 0
    for m in range(12):
        shift = 32 if m % 2 == 0 else 96
        if m < 2:
            rolled = pltpu.roll(lines, shift, 1)
            if m == 0:
                even = rolled
            else:
                odd = rolled
        source = even if m % 2 == 0 else odd
        at = (64 * m - 32 + shift) % 768
        part = jnp.where(lane0, first, source[:, at : at + 128])
        high, low = split(part)
        left[m * rows : (m + 1) * rows, 0:128] = high
        left[m * rows : (m + 1) * rows, 128:256] = low


def row_start(row):
    return (row // TILE) * GROUP + row % TILE


def spread(left, matrix, columns, rows, store):
    res = jnp.dot(left, matrix[:, columns], preferred_element_type=jnp.float32)
    for m in range(12):
        for h in range(2):
            for t in range(rows // TILE):
                at = m * rows + t * TILE
                store(t, 2 * m + h, res[at : at + TILE, LANES * h : LANES * h + LANES])


def fine_fields(gx, gy, left_x, left_y, coefs, ylines, matrix, rows_matrix):
    high, low = split(gx)
    lines = jnp.dot(rows_matrix[...], jnp.concatenate([high, low], axis=0), preferred_element_type=jnp.float32)
    windows(0.8 * lines, left_x, 1.0)
    windows(1.6 * gy, left_y, 0.0)
    for q in range(4):

        def store(t, seg, values):
            coefs[q, pl.ds((t * SEGMENTS + seg) * TILE, TILE), :] = values

        spread(left_x[...], matrix, slice(256 * q, 256 * q + 256), lines.shape[0], store)

    def store_y(t, seg, values):
        if t < ylines.shape[0] // GROUP:
            ylines[pl.ds((t * SEGMENTS + seg) * TILE, TILE), :] = values

    spread(left_y[...], matrix, slice(0, 256), gy.shape[0], store_y)


def row_at(row):
    return pl.ds((row // TILE) * GROUP + row % TILE, SEGMENTS, stride=TILE)


def x_swept(coefs, at, value, lane):
    v, s, dp, dm = (coefs[q, at, :] for q in range(4))
    parts = products(value, s + v * jnp.where(v >= 0.0, dp, dm))
    total = parts[4]
    ahead = behind = None
    for s in range(1, 5):
        raised = pltpu.roll(parts[4 + s], s, 1)
        over = jnp.where(lane < s, raised, 0.0)
        ahead = over if ahead is None else ahead + over
        lowered = pltpu.roll(parts[4 - s], LANES - s, 1)
        under = jnp.where(lane >= LANES - s, lowered, 0.0)
        behind = under if behind is None else behind + under
        total = total + (raised + lowered)
    total = total - (ahead + behind)
    return total + (pltpu.roll(ahead, 1, 0) + pltpu.roll(behind, SEGMENTS - 1, 0))


def y_products(ylines, cell, source):
    below, here, above = (ylines[row_at(cell + k), :] for k in (-1, 0, 1))
    dm, dp = here - below, above - here
    for r in range(4):
        v0 = (r - 1.5) / 4
        u0 = here + v0 * (dp if v0 > 0 else dm)
        v = v0 + 0.5 * u0
        yield products(source(r), (u0 + here) + v * jnp.where(v >= 0.0, dp, dm))


def lanes():
    return lax.broadcasted_iota(jnp.int32, (SEGMENTS, LANES), 1)


def inner_kernel(got, scalar, matrix, rows_matrix, out, partial, gx, gy, left_x, left_y, coefs, ylines, moved, done, sems):
    for j in range(16):
        gx[:, 48 * j : 48 * j + 48] = got[j, :, 0:48]
        gy[:, 48 * j : 48 * j + 48] = got[j, :, 64:112]
    fine_fields(gx[...], gy[...], left_x, left_y, coefs, ylines, matrix, rows_matrix)
    lane = lanes()

    def x_rows(block, carry):
        for r in range(4):
            row = block * 4 + r
            at = row_at(row)
            moved[row] = x_swept(coefs, at, scalar[at, :], lane)
        return carry

    lax.fori_loop(0, 12, x_rows, 0)

    def y_cell(cell, carry):
        acc = list(carry) + [None] * 4
        for r, parts in enumerate(y_products(ylines, cell, lambda r: moved[cell * 4 + r])):
            for s in range(9):
                acc[r + s] = parts[s] if acc[r + s] is None else acc[r + s] + parts[s]
        return acc

    zero = jnp.zeros((SEGMENTS, LANES), jnp.float32)

    def first_cell(cell, carry):
        acc = y_cell(cell, carry)
        for r in range(4):
            partial[4 * (cell - 1) + r] = acc[r]
        return tuple(acc[4:])

    carry = lax.fori_loop(1, 3, first_cell, (zero,) * 8)

    def tile_copy(tile):
        at = pl.ds(tile * GROUP, GROUP)
        return pltpu.make_async_copy(done.at[at, :], out.at[at, :], sems.at[tile])

    for tile in range(1, 5):

        def cell_rows(cell, carry):
            acc = y_cell(cell, carry)
            for r in range(4):
                done[row_at(4 * cell - 4 + r), :] = acc[r]
            return tuple(acc[4:])

        carry = lax.fori_loop(2 * tile + 1, 2 * tile + 3, cell_rows, carry)
        tile_copy(tile).start()
    for r in range(8):
        partial[8 + r] = carry[r]
    for tile in range(1, 5):
        tile_copy(tile).wait()


def edge_kernel(got, below, above, scalar, top, bottom, partial, matrix, rows_matrix, inner, out, gx, gy, left_x, left_y, coefs, ylines, moved, done, sems):
    del inner
    gy[8:16, :] = jnp.zeros((8, 768), jnp.float32)
    for j in range(16):
        at = slice(48 * j, 48 * j + 48)
        for row, ref in ((0, below[j]), (2, got[j, 0:2, :]), (4, got[j, 10:12, :]), (6, above[j])):
            gx[row : row + 2, at] = ref[:, 0:48]
            gy[row : row + 2, at] = ref[:, 64:112]
    fine_fields(gx[...], gy[...], left_x, left_y, coefs, ylines, matrix, rows_matrix)
    lane = lanes()
    sources = [(top, 4), (scalar, 0), (scalar, 44), (bottom, 0)]
    for i in range(16):
        ref, first = sources[i // 4]
        moved[i] = x_swept(coefs, row_at(i), ref[row_at(first + i % 4), :], lane)
    for side, (cells, tile) in enumerate((((-1, 0), 0), ((11, 12), 5))):
        acc = {8 * tile + r: partial[8 * side + r] for r in range(8)}
        for k, c in enumerate(cells):
            for r, parts in enumerate(y_products(ylines, EDGE_CELLS.index(c), lambda r: moved[8 * side + 4 * k + r])):
                for s in range(9):
                    row = 4 * c + r + s - 4
                    if row in acc:
                        acc[row] = acc[row] + parts[s]
        for r in range(8):
            done[row_at(8 * side + r), :] = acc[8 * tile + r]
        pltpu.make_async_copy(
            done.at[pl.ds(side * GROUP, GROUP), :], out.at[pl.ds(tile * GROUP, GROUP), :], sems.at[side]
        ).start()
    for side, tile in ((0, 0), (1, 5)):
        pltpu.make_async_copy(
            done.at[pl.ds(side * GROUP, GROUP), :], out.at[pl.ds(tile * GROUP, GROUP), :], sems.at[side]
        ).wait()


def scratch(rows, cells, ytiles, done_tiles):
    return [
        pltpu.VMEM((cells, 768), jnp.float32),
        pltpu.VMEM((16, 768), jnp.float32),
        pltpu.VMEM((12 * rows, 256), jnp.bfloat16),
        pltpu.VMEM((12 * 16, 256), jnp.bfloat16),
        pltpu.VMEM((4, rows // TILE * GROUP, LANES), jnp.float32),
        pltpu.VMEM((ytiles * GROUP, LANES), jnp.float32),
        pltpu.VMEM((rows, SEGMENTS, LANES), jnp.float32),
        pltpu.VMEM((done_tiles * GROUP, LANES), jnp.float32),
    ]


VMEM_SPEC = pl.BlockSpec(memory_space=pltpu.VMEM)
ANY_SPEC = pl.BlockSpec(memory_space=pl.ANY)
PARAMS = pltpu.CompilerParams(vmem_limit_bytes=32 * 2**20)


def inner_sweeps(got, scalar, matrix):
    return pl.pallas_call(
        inner_kernel,
        out_shape=(
            jax.ShapeDtypeStruct((6 * GROUP, LANES), jnp.float32),
            jax.ShapeDtypeStruct((16, SEGMENTS, LANES), jnp.float32),
        ),
        in_specs=[VMEM_SPEC] * 4,
        out_specs=(ANY_SPEC, VMEM_SPEC),
        scratch_shapes=scratch(48, 16, 2, 6) + [pltpu.SemaphoreType.DMA((6,))],
        compiler_params=PARAMS,
        cost_estimate=pl.CostEstimate(flops=4 * 10**7, bytes_accessed=16 * 2**20, transcendentals=0),
        name="inner_sweeps",
    )(got, scalar, matrix, jnp.asarray(row_matrix(INNER_ROWS, INNER_CELLS), jnp.bfloat16))


def edge_sweeps(got, below, above, scalar, top, bottom, partial, matrix, inner):
    return pl.pallas_call(
        edge_kernel,
        out_shape=jax.ShapeDtypeStruct((6 * GROUP, LANES), jnp.float32),
        in_specs=[VMEM_SPEC] * 9 + [ANY_SPEC],
        out_specs=ANY_SPEC,
        scratch_shapes=scratch(16, 8, 1, 2) + [pltpu.SemaphoreType.DMA((2,))],
        input_output_aliases={9: 0},
        compiler_params=PARAMS,
        name="edge_sweeps",
    )(got, below, above, scalar, top, bottom, partial, matrix, jnp.asarray(row_matrix(EDGE_ROWS, EDGE_CELLS), jnp.bfloat16), inner)


def local(scalar, x_velocity, y_velocity):
    count = lax.axis_size("row")
    up = [(i, (i + 1) % count) for i in range(count)]
    down = [((i + 1) % count, i) for i in range(count)]
    tiles = scalar.reshape(6, TILE, SEGMENTS, LANES).transpose(0, 2, 1, 3).reshape(6 * GROUP, LANES)
    matrix = jnp.asarray(interp_matrices(), jnp.bfloat16)
    top = lax.ppermute(tiles[5 * GROUP :], "row", up)
    bottom = lax.ppermute(tiles[:GROUP], "row", down)
    got = lax.all_to_all(pack(x_velocity, y_velocity), "line", 0, 0, tiled=True)
    below = lax.ppermute(got[:, 10:12], "row", up)
    above = lax.ppermute(got[:, 0:2], "row", down)
    inner, partial = inner_sweeps(got, tiles, matrix)
    result = edge_sweeps(got, below, above, tiles, top, bottom, partial, matrix, inner)
    return result.reshape(6, SEGMENTS, TILE, LANES).transpose(0, 2, 1, 3).reshape(1, 48, 3072)


def solution(mesh):
    in_specs = (P("line", "row", None), P(None, "row", "line"), P(None, "row", "line"))
    out_specs = P("line", "row", None)
    return jax.shard_map(local, mesh=mesh, in_specs=in_specs, out_specs=out_specs, check_vma=False)
```

time: 38.4 us -> 36.2 us (0.943)
  waiting for transfers between devices: 10.6 us -> 6.77 us
  other arithmetic: 1.71 us -> 0 us
  local copies, waits for them, and re-layouts: 0.67 us -> 2.02 us
  Pallas kernels: 8.56 us -> 9.73 us
  starting transfers between devices: 16.3 us -> 17.3 us
    ppermute x2, waiting for transfers between devices: 2.47 us -> 0.01 us  [the longest x1 0.01 us: local(): above = lax.ppermute(got[:, 0:2], 'row', down)]
    ppermute x1, waiting for transfers between devices: 2.3 us -> 0.01 us  [local(): bottom = lax.ppermute(tiles[:GROUP], 'row', down)]
    all_to_all x1, waiting for transfers between devices: 5.17 us -> 6.76 us  [local(): got = lax.all_to_all(pack(x_velocity, y_velocity), 'line', 0, 0, tiled=True)]
    pallas_call x1 -> x2, Pallas kernels: 6.99 us -> 8.1 us  [the longest x1 5.76 us: inner_sweeps(): pl.pallas_call(inner_kernel, out_shape=(jax.ShapeDtypeStruct((6 * GROUP,...]
    unnamed x6 -> x8, local copies, waits for them, and re-layouts: 0.02 us -> 1.05 us
    slice x1, local copies, waits for them, and re-layouts: 0.02 us -> 0.96 us  [local(): bottom = lax.ppermute(tiles[:GROUP], 'row', down)]
    slice x1 -> x0, other arithmetic: 0.86 us -> none  [local(): low = lax.ppermute(pair[:, :, 10:], 'row', up)]
    concatenate x1 -> x0, other arithmetic: 0.85 us -> none  [local(): pair = jnp.concatenate([low, pair, high], axis=2)]
  transfers between devices with their start and end apart: 5 -> 5, of which waited for: 5 -> 1; matrix products, arithmetic and copies ran while one was open for 0% -> 3% of each run, Pallas kernels for 0% -> 16%
where the time goes in v2:
time: 36.2 us; the launch traced here: 35.9 us
  starting transfers between devices  17.3 us (48%)
  Pallas kernels  9.73 us (27%)
  waiting for transfers between devices  6.77 us (19%)
  local copies, waits for them, and re-layouts  2.02 us (6%)
    all_to_all x1, starting transfers between devices, local(): got = lax.all_to_all(pack(x_velocity, y_velocity), 'line', 0, 0, tiled=True)  11.6 us
    all_to_all x1, waiting for transfers between devices, local(): got = lax.all_to_all(pack(x_velocity, y_velocity), 'line', 0, 0, tiled=True)  6.76 us
    pallas_call x1, Pallas kernels, inner_sweeps(): pl.pallas_call(inner_kernel, out_shape=(jax.ShapeDtypeStruct((6 * GROUP,...  5.76 us
    pallas_call x1, Pallas kernels, edge_sweeps(): pl.pallas_call(edge_kernel, out_shape=jax.ShapeDtypeStruct((6 * GROUP, LA...  2.34 us
    ppermute x1, starting transfers between devices, local(): above = lax.ppermute(got[:, 0:2], 'row', down)  2.13 us
    pallas_call x1, Pallas kernels, pack(): pl.pallas_call(pack_kernel, out_shape=jax.ShapeDtypeStruct((16, 16, 128),...  1.63 us
    ppermute x1, starting transfers between devices, local(): top = lax.ppermute(tiles[5 * GROUP:], 'row', up)  1.27 us
    ppermute x1, starting transfers between devices, local(): below = lax.ppermute(got[:, 10:12], 'row', up)  1.27 us
  transfers between devices with their start and end apart: 5, of which 1 were waited for; matrix products, arithmetic and copies ran while one was open for 3% of the time, Pallas kernels for 16%

profile of v2, /device:TPU:1, one launch (start us, length us, event | category | flops | bytes accessed | tf_op | source)
XLA Modules:
  0.0 35.9 jit_solution(10433050473440893857)
XLA Ops:
  0.0 0.0 copy-start
  0.0 1.6 %pack_planes.1 = f32[16,16,128]{2,1,0:T(8,128)} custom-call(f32[6,12,48]{2,1,0:T(8,128)} %x_ref.1, f32[6,12,48]{2,1,0:T(8,128)} %y_ref.1), custom_call_target="tpu_custom_call" | custom-call | tf_op jit(solution)/shard_map/pack_planes/pallas_call | solution.py:110
  1.6 11.6 %all-to-all-start = ((f32[16,16,128]{2,1,0:T(8,128)}), f32[16,16,128]{2,1,0:T(8,128)S(1)}, u32[]{:S(2)}, u32[]{:S(2)}) async-start(f32[16,16,128]{2,1,0:T(8,128)} %pack_planes.1), calls=%async_computation | async-start | bytes 262144 | tf_op jit(solution)/shard_map/all_to_all | solution.py:351
  13.2 1.0 %slice_bitcast_fusion = (f32[192,128]{1,0:T(8,128)S(1)}, f32[192,128]{1,0:T(8,128)S(1)}) fusion(f32[6,24,8,128]{3,2,1,0:T(8,128)} %bitcast.14), kind=kLoop, calls=%fused_computation | loop fusion | bytes 393216 | tf_op jit(solution)/shard_map/slice | solution.py:350
  14.2 1.0 %collective-permute-start.3 = (f32[192,128]{1,0:T(8,128)S(1)}, f32[192,128]{1,0:T(8,128)S(1)}, u32[]{:S(2)}, u32[]{:S(2)}) collective-permute-start(f32[192,128]{1,0:T(8,128)S(1)} %get-tuple-element.9), channel_id=1, source_target_pairs={{16,0},{32,16},{48,32},{64,48},{80,64},{96,80},{112,96},{128,112},... | collective-permute-start | bytes 294920 | tf_op jit(solution)/shard_map/ppermute | solution.py:350
  15.2 1.3 %collective-permute-start.2 = (f32[192,128]{1,0:T(8,128)S(1)}, f32[192,128]{1,0:T(8,128)S(1)}, u32[]{:S(2)}, u32[]{:S(2)}) collective-permute-start(f32[192,128]{1,0:T(8,128)S(1)} %get-tuple-element.10), channel_id=1, source_target_pairs={{0,16},{16,32},{32,48},{48,64},{64,80},{80,96},{96,112},{112,128},... | collective-permute-start | bytes 294920 | tf_op jit(solution)/shard_map/ppermute | solution.py:349
  16.5 6.8 %all-to-all-done.got = f32[16,16,128]{2,1,0:T(8,128)S(1)} async-done(((f32[16,16,128]{2,1,0:T(8,128)}), f32[16,16,128]{2,1,0:T(8,128)S(1)}, u32[]{:S(2)}, u32[]{:S(2)}) %all-to-all-start) | async-done | bytes 131104 | tf_op jit(solution)/shard_map/all_to_all | solution.py:351
  23.2 0.0 copy-start.2
  23.3 2.1 %collective-permute-start.1 = (f32[16,2,128]{2,1,0:T(2,128)S(1)}, f32[16,2,128]{2,1,0:T(2,128)S(1)}, u32[]{:S(2)}, u32[]{:S(2)}) collective-permute-start(f32[16,2,128]{2,1,0:T(2,128)S(1)} %get-tuple-element.11), channel_id=1, source_target_pairs={{16,0},{32,16},{48,32},{64,48},{80,64},{96,80},{112,96},{128,112},... | collective-permute-start | bytes 49160 | tf_op jit(solution)/shard_map/ppermute | solution.py:353
  25.4 1.3 %collective-permute-start = (f32[16,2,128]{2,1,0:T(2,128)S(1)}, f32[16,2,128]{2,1,0:T(2,128)S(1)}, u32[]{:S(2)}, u32[]{:S(2)}) collective-permute-start(f32[16,2,128]{2,1,0:T(2,128)S(1)} %get-tuple-element.12), channel_id=1, source_target_pairs={{0,16},{16,32},{32,48},{48,64},{64,80},{80,96},{96,112},{112,128},... | collective-permute-start | bytes 49160 | tf_op jit(solution)/shard_map/ppermute | solution.py:352
  26.7 0.0 copy-done
  26.7 0.0 copy-done.2
  26.7 0.0 copy-start.1
  26.7 1.0 %copy-done.1 = bf16[256,1024]{1,0:T(8,128)(2,1)S(1)} copy-done((bf16[256,1024]{1,0:T(8,128)(2,1)S(1)}, bf16[256,1024]{1,0:T(8,128)(2,1)}, u32[]{:S(2)}) %copy-start.1) | copy-done | bytes 524312
  27.7 0.0 copy-start.3
  27.7 5.8 %inner_sweeps.1 = (f32[1152,128]{1,0:T(8,128)}, f32[16,24,128]{2,1,0:T(8,128)S(1)}) custom-call(f32[16,16,128]{2,1,0:T(8,128)S(1)} %all-to-all-done.got, f32[1152,128]{1,0:T(8,128)S(1)} %bitcast.15, bf16[256,1024]{1,0:T(8,128)(2,1)S(1)} %copy-done.1, bf16[48,32]{1,0:T(8,128)(2,1)S(1)} %copy-done.2), custom_call_target="tpu_custom_call" | custom-call | flops 40000000 | bytes 16777216 | tf_op jit(solution)/shard_map/inner_sweeps/pallas_call | solution.py:315
  33.5 0.0 collective-permute-done.3.bottom
  33.5 0.0 collective-permute-done.2.top
  33.5 0.0 collective-permute-done.1.above
  33.5 0.0 collective-permute-done.below
  33.5 0.0 copy-done.3
  33.5 2.3 %edge_sweeps.1 = f32[1152,128]{1,0:T(8,128)} custom-call(f32[16,16,128]{2,1,0:T(8,128)S(1)} %all-to-all-done.got, f32[16,2,128]{2,1,0:T(2,128)S(1)} %collective-permute-done.below, f32[16,2,128]{2,1,0:T(2,128)S(1)} %collective-permute-done.1.above, f32[1152,128]{1,0:T(8,128)S(1)} %bitcast.16, ...), custom_call_target="tpu_custom_call", output_to_operand_aliasing={{}: (9, {})} | custom-call | tf_op jit(solution)/shard_map/edge_sweeps/pallas_call | solution.py:331
  (1 shorter events, 0.0 us)
Async XLA Ops:
  0.0 26.7 %copy-start = (f32[1,48,3072]{2,1,0:T(8,128)S(1)}, f32[1,48,3072]{2,1,0:T(8,128)}, u32[]{:S(2)}) copy-start(f32[1,48,3072]{2,1,0:T(8,128)} %param.6) | copy-start | bytes 1769476
  1.6 21.6 %all-to-all-start = ((f32[16,16,128]{2,1,0:T(8,128)}), f32[16,16,128]{2,1,0:T(8,128)S(1)}, u32[]{:S(2)}, u32[]{:S(2)}) async-start(f32[16,16,128]{2,1,0:T(8,128)} %pack_planes.1), calls=%async_computation | async-start | bytes 262144 | tf_op jit(solution)/shard_map/all_to_all | solution.py:351
  14.2 19.3 %collective-permute-start.3 = (f32[192,128]{1,0:T(8,128)S(1)}, f32[192,128]{1,0:T(8,128)S(1)}, u32[]{:S(2)}, u32[]{:S(2)}) collective-permute-start(f32[192,128]{1,0:T(8,128)S(1)} %get-tuple-element.9), channel_id=1, source_target_pairs={{16,0},{32,16},{48,32},{64,48},{80,64},{96,80},{112,96},{128,112},... | collective-permute-start | bytes 294920 | tf_op jit(solution)/shard_map/ppermute | solution.py:350
  15.2 18.3 %collective-permute-start.2 = (f32[192,128]{1,0:T(8,128)S(1)}, f32[192,128]{1,0:T(8,128)S(1)}, u32[]{:S(2)}, u32[]{:S(2)}) collective-permute-start(f32[192,128]{1,0:T(8,128)S(1)} %get-tuple-element.10), channel_id=1, source_target_pairs={{0,16},{16,32},{32,48},{48,64},{64,80},{80,96},{96,112},{112,128},... | collective-permute-start | bytes 294920 | tf_op jit(solution)/shard_map/ppermute | solution.py:349
  23.2 3.4 %copy-start.2 = (bf16[48,32]{1,0:T(8,128)(2,1)S(1)}, bf16[48,32]{1,0:T(8,128)(2,1)}, u32[]{:S(2)}) copy-start(bf16[48,32]{1,0:T(8,128)(2,1)} %constant.7.clone.rows_matrix) | copy-start | bytes 9220
  23.3 10.2 %collective-permute-start.1 = (f32[16,2,128]{2,1,0:T(2,128)S(1)}, f32[16,2,128]{2,1,0:T(2,128)S(1)}, u32[]{:S(2)}, u32[]{:S(2)}) collective-permute-start(f32[16,2,128]{2,1,0:T(2,128)S(1)} %get-tuple-element.11), channel_id=1, source_target_pairs={{16,0},{32,16},{48,32},{64,48},{80,64},{96,80},{112,96},{128,112},... | collective-permute-start | bytes 49160 | tf_op jit(solution)/shard_map/ppermute | solution.py:353
  25.4 8.1 %collective-permute-start = (f32[16,2,128]{2,1,0:T(2,128)S(1)}, f32[16,2,128]{2,1,0:T(2,128)S(1)}, u32[]{:S(2)}, u32[]{:S(2)}) collective-permute-start(f32[16,2,128]{2,1,0:T(2,128)S(1)} %get-tuple-element.12), channel_id=1, source_target_pairs={{0,16},{16,32},{32,48},{48,64},{64,80},{80,96},{96,112},{112,128},... | collective-permute-start | bytes 49160 | tf_op jit(solution)/shard_map/ppermute | solution.py:352
  26.7 1.0 %copy-start.1 = (bf16[256,1024]{1,0:T(8,128)(2,1)S(1)}, bf16[256,1024]{1,0:T(8,128)(2,1)}, u32[]{:S(2)}) copy-start(bf16[256,1024]{1,0:T(8,128)(2,1)} %constant.6.clone.matrix) | copy-start | bytes 1572868
  27.7 5.8 %copy-start.3 = (bf16[16,16]{1,0:T(8,128)(2,1)S(1)}, bf16[16,16]{1,0:T(8,128)(2,1)}, u32[]{:S(2)}) copy-start(bf16[16,16]{1,0:T(8,128)(2,1)} %constant.8.clone.rows_matrix) | copy-start | bytes 1540

commit v3 on v2

v3 whole, which is shorter than its diff:
```python
import functools

import jax
import jax.numpy as jnp
import numpy as np
from jax import lax
from jax.experimental import pallas as pl
from jax.experimental.pallas import tpu as pltpu
from jax.sharding import PartitionSpec as P

SEGMENTS, LANES, TILE = 24, 128, 8
GROUP = SEGMENTS * TILE
WINDOW = 64


def kernel_parts():
    a = np.polynomial.Polynomial([0.0, 1.0])
    pieces = (
        -(a - 1) * (25 * a**4 - 38 * a**3 - 3 * a**2 + 12 * a + 12) / 12,
        (a - 1) * (a - 2) * (25 * a**3 - 114 * a**2 + 153 * a - 48) / 24,
        -(a - 2) * (a - 3) ** 3 * (5 * a - 8) / 24,
    )
    parts = []
    for middle, piece in zip((0.5, 1.5, 2.5), pieces):
        coefs = piece(middle - a).coef
        parts.append(([float(c) for c in coefs[0::2]], [float(c) for c in coefs[1::2]]))
    return parts


PARTS = kernel_parts()


def products(value, d):
    high = d >= 0.0
    e = d - jnp.where(high, 1.0, -1.0)
    right = e >= 0.0
    t = jnp.abs(e) - 0.5
    tau = t * t
    vt = value * t
    evens, odds = [None], [None]
    for even, odd in PARTS[1:]:
        evens.append(value * ((even[2] * tau + even[1]) * tau + even[0]))
        odds.append(vt * ((odd[2] * tau + odd[1]) * tau + odd[0]))
    evens[0] = 0.5 * value - (evens[1] + evens[2])
    odds[0] = vt - (3.0 * odds[1] + 5.0 * odds[2])
    near = [ev + od for ev, od in zip(evens, odds)]
    far = [ev - od for ev, od in zip(evens, odds)]
    q = {0: far[0]}
    q[1] = jnp.where(right, near[0], far[1])
    q[-1] = jnp.where(right, far[1], near[0])
    q[2] = jnp.where(right, near[1], far[2])
    q[-2] = jnp.where(right, far[2], near[1])
    q[3] = jnp.where(right, near[2], 0.0)
    q[-3] = jnp.where(right, 0.0, near[2])
    out = []
    for s in range(-4, 5):
        up, down = q.get(s - 1), q.get(s + 1)
        out.append(jnp.where(high, 0.0 if up is None else up, 0.0 if down is None else down))
    return out


def fill_matrix(out):
    row = lax.broadcasted_iota(jnp.int32, (128, 256), 0)
    fine = lax.broadcasted_iota(jnp.int32, (128, 256), 1)
    offset = row - 32 - (fine >> 2)
    v = ((fine & 3).astype(jnp.float32) - 1.5) * 0.25
    size = jnp.abs(v)
    own = jnp.where(offset == 0, 1.0, 0.0)
    next_cell = jnp.where(offset == 1, 1.0, 0.0)
    last_cell = jnp.where(offset == -1, 1.0, 0.0)
    value = own * (1.0 - size) + jnp.where(v > 0, next_cell, last_cell) * size
    low = 0.5 * value
    blocks = (jnp.where(row == 0, v, low), value + own, next_cell - own, own - last_cell)
    for q, block in enumerate(blocks):
        block = block.astype(jnp.bfloat16)
        out[0:128, 256 * q : 256 * q + 256] = block
        out[128:256, 256 * q : 256 * q + 256] = block if q else low.astype(jnp.bfloat16)


def row_matrix(fine_rows, coarse_rows):
    a = np.zeros((len(fine_rows), len(coarse_rows)))
    for i, y in enumerate(fine_rows):
        c, v = y // 4, (y % 4 - 1.5) / 4
        for cell, weight in ((c, 1 - abs(v)), (c + (1 if v > 0 else -1), abs(v))):
            if cell in coarse_rows:
                a[i, coarse_rows.index(cell)] += weight
    return np.concatenate([a, a], axis=1)


INNER_ROWS, INNER_CELLS = list(range(48)), list(range(12)) + [None] * 4
EDGE_ROWS = list(range(-4, 4)) + list(range(44, 52))
EDGE_CELLS = [-2, -1, 0, 1, 10, 11, 12, 13] + [None] * 8


def pack_kernel(x_ref, y_ref, out_ref, both):
    both[...] = jnp.zeros_like(both)
    both[:, :, 0:48] = x_ref[...]
    both[:, :, 64:112] = y_ref[...]
    for k in range(16):
        q, w = (k + 2) // 4, ((k + 2) % 4 + 0.5) / 4
        out_ref[k] = (1 - w) * both[q] + w * both[q + 1]


def pack(x, y):
    return pl.pallas_call(
        pack_kernel,
        out_shape=jax.ShapeDtypeStruct((16, 12, 128), jnp.float32),
        scratch_shapes=[pltpu.VMEM((6, 12, 128), jnp.float32)],
        name="pack_planes",
    )(x, y)


def split(values):
    high = values.astype(jnp.bfloat16)
    low = (values - high.astype(jnp.float32)).astype(jnp.bfloat16)
    return high, low


def windows(lines, left, first):
    rows = lines.shape[0]
    lane0 = lax.broadcasted_iota(jnp.int32, (rows, 128), 1) == 0
    for m in range(12):
        shift = 32 if m % 2 == 0 else 96
        if m < 2:
            rolled = pltpu.roll(lines, shift, 1)
            if m == 0:
                even = rolled
            else:
                odd = rolled
        source = even if m % 2 == 0 else odd
        at = (64 * m - 32 + shift) % 768
        part = jnp.where(lane0, first, source[:, at : at + 128])
        high, low = split(part)
        left[m * rows : (m + 1) * rows, 0:128] = high
        left[m * rows : (m + 1) * rows, 128:256] = low


def row_start(row):
    return (row // TILE) * GROUP + row % TILE


def spread(left, matrix, columns, rows, store):
    res = jnp.dot(left, matrix[:, columns], preferred_element_type=jnp.float32)
    for m in range(12):
        for h in range(2):
            for t in range(rows // TILE):
                at = m * rows + t * TILE
                store(t, 2 * m + h, res[at : at + TILE, LANES * h : LANES * h + LANES])


def fine_fields(gx, gy, left_x, left_y, coefs, ylines, matrix, rows_matrix):
    high, low = split(gx)
    lines = jnp.dot(rows_matrix[...], jnp.concatenate([high, low], axis=0), preferred_element_type=jnp.float32)
    windows(0.8 * lines, left_x, 1.0)
    windows(1.6 * gy, left_y, 0.0)
    for q in range(4):

        def store(t, seg, values):
            coefs[q, pl.ds((t * SEGMENTS + seg) * TILE, TILE), :] = values

        spread(left_x[...], matrix, slice(256 * q, 256 * q + 256), lines.shape[0], store)

    def store_y(t, seg, values):
        if t < ylines.shape[0] // GROUP:
            ylines[pl.ds((t * SEGMENTS + seg) * TILE, TILE), :] = values

    spread(left_y[...], matrix, slice(0, 256), gy.shape[0], store_y)


def row_at(row):
    return pl.ds((row // TILE) * GROUP + row % TILE, SEGMENTS, stride=TILE)


def x_swept(coefs, at, value, lane):
    v, s, dp, dm = (coefs[q, at, :] for q in range(4))
    parts = products(value, s + v * jnp.where(v >= 0.0, dp, dm))
    total, wrap = parts[4], None
    for s in range(1, 5):
        raised = pltpu.roll(parts[4 + s], s, 1)
        lowered = pltpu.roll(parts[4 - s], LANES - s, 1)
        over = jnp.where(lane < s, raised, jnp.where(lane >= LANES - s, lowered, 0.0))
        wrap = over if wrap is None else wrap + over
        total = total + (raised + lowered)
    moved_wrap = jnp.where(lane < LANES // 2, pltpu.roll(wrap, 1, 0), pltpu.roll(wrap, SEGMENTS - 1, 0))
    return (total - wrap) + moved_wrap


def y_products(ylines, cell, source):
    below, here, above = (ylines[row_at(cell + k), :] for k in (-1, 0, 1))
    dm, dp = here - below, above - here
    for r in range(4):
        v0 = (r - 1.5) / 4
        u0 = here + v0 * (dp if v0 > 0 else dm)
        v = v0 + 0.5 * u0
        yield products(source(r), (u0 + here) + v * jnp.where(v >= 0.0, dp, dm))


def lanes():
    return lax.broadcasted_iota(jnp.int32, (SEGMENTS, LANES), 1)


KEPT = (2, 3, 44, 45)


def inner_kernel(got, scalar, rows_matrix, done, partial, kept, matrix, gx, gy, left_x, left_y, coefs, ylines, moved):
    gx[8:16, :] = jnp.zeros((8, 768), jnp.float32)
    gy[8:16, :] = jnp.zeros((8, 768), jnp.float32)
    for j in range(16):
        gx[0:12, 48 * j : 48 * j + 48] = got[j, :, 0:48]
        gy[0:12, 48 * j : 48 * j + 48] = got[j, :, 64:112]
    fill_matrix(matrix)
    fine_fields(gx[...], gy[...], left_x, left_y, coefs, ylines, matrix, rows_matrix[0:48, :])
    lane = lanes()

    def x_rows(block, carry):
        for r in range(22):
            row = block * 22 + r + 2
            at = row_at(row)
            moved[row] = x_swept(coefs, at, scalar[at, :], lane)
        return carry

    lax.fori_loop(0, 2, x_rows, 0)
    for i, row in enumerate(KEPT):
        kept[i] = moved[row]

    def y_cell(cell, acc):
        acc = acc + [None] * 4
        for r, parts in enumerate(y_products(ylines, cell, lambda r: moved[cell * 4 + r])):
            for s in range(9):
                acc[r + s] = parts[s] if acc[r + s] is None else acc[r + s] + parts[s]
        return acc

    acc = [None] * 8
    for cell in (1, 2):
        acc = y_cell(cell, acc)
        for r in range(4):
            partial[4 * (cell - 1) + r] = acc[r]
        acc = acc[4:]

    for cell in range(3, 11):
        acc = y_cell(cell, acc)
        for r in range(4):
            done[row_at(4 * cell - 12 + r), :] = acc[r]
        acc = acc[4:]
    for r in range(8):
        partial[8 + r] = acc[r]


def edge_kernel(odd_ref, got, line_a, line_b, scalar, tile_a, tile_b, partial, kept, matrix, done, rows_matrix, out, gx, gy, left_x, left_y, coefs, ylines, moved, edge, sems):
    inner_copy = pltpu.make_async_copy(done, out.at[pl.ds(GROUP, 4 * GROUP), :], sems.at[2])
    inner_copy.start()
    gx[8:16, :] = jnp.zeros((8, 768), jnp.float32)
    odd = odd_ref[0] == 1
    gy[8:16, :] = jnp.zeros((8, 768), jnp.float32)
    for j in range(16):
        at = slice(48 * j, 48 * j + 48)
        from_a, from_b = line_a[j], line_b[j]
        below, above = jnp.where(odd, from_a, from_b), jnp.where(odd, from_b, from_a)
        for row, values in ((0, below), (2, got[j, 0:2, :]), (4, got[j, 10:12, :]), (6, above)):
            gx[row : row + 2, at] = values[:, 0:48]
            gy[row : row + 2, at] = values[:, 64:112]
    fine_fields(gx[...], gy[...], left_x, left_y, coefs, ylines, matrix, rows_matrix[48:64, :])
    lane = lanes()
    for i, y in enumerate(EDGE_ROWS):
        if y in KEPT:
            moved[i] = kept[KEPT.index(y)]
            continue
        if 0 <= y < 48:
            value = scalar[row_at(y), :]
        else:
            at = row_at(y % TILE)
            from_a, from_b = tile_a[at, :], tile_b[at, :]
            value = jnp.where(odd, from_a, from_b) if y < 0 else jnp.where(odd, from_b, from_a)
        moved[i] = x_swept(coefs, row_at(i), value, lane)

    def tile_copy(side, tile):
        return pltpu.make_async_copy(
            edge.at[pl.ds(side * GROUP, GROUP), :], out.at[pl.ds(tile * GROUP, GROUP), :], sems.at[side]
        )

    for side, (cells, tile) in enumerate((((-1, 0), 0), ((11, 12), 5))):
        acc = {8 * tile + r: partial[8 * side + r] for r in range(8)}
        for k, c in enumerate(cells):
            for r, parts in enumerate(y_products(ylines, EDGE_CELLS.index(c), lambda r: moved[8 * side + 4 * k + r])):
                for s in range(9):
                    row = 4 * c + r + s - 4
                    if row in acc:
                        acc[row] = acc[row] + parts[s]
        for r in range(8):
            edge[row_at(8 * side + r), :] = acc[8 * tile + r]
        tile_copy(side, tile).start()
    inner_copy.wait()
    tile_copy(0, 0).wait()
    tile_copy(1, 5).wait()


def scratch(rows, ytiles):
    return [
        pltpu.VMEM((16, 768), jnp.float32),
        pltpu.VMEM((16, 768), jnp.float32),
        pltpu.VMEM((12 * rows, 256), jnp.bfloat16),
        pltpu.VMEM((12 * 16, 256), jnp.bfloat16),
        pltpu.VMEM((4, rows // TILE * GROUP, LANES), jnp.float32),
        pltpu.VMEM((ytiles * GROUP, LANES), jnp.float32),
        pltpu.VMEM((rows, SEGMENTS, LANES), jnp.float32),
    ]


VMEM_SPEC = pl.BlockSpec(memory_space=pltpu.VMEM)
ANY_SPEC = pl.BlockSpec(memory_space=pl.ANY)
PARAMS = pltpu.CompilerParams(vmem_limit_bytes=32 * 2**20)


def rows_matrices():
    return jnp.asarray(
        np.concatenate([row_matrix(INNER_ROWS, INNER_CELLS), row_matrix(EDGE_ROWS, EDGE_CELLS)]), jnp.bfloat16
    )


def inner_sweeps(got, scalar, rows_matrix):
    return pl.pallas_call(
        inner_kernel,
        out_shape=(
            jax.ShapeDtypeStruct((4 * GROUP, LANES), jnp.float32),
            jax.ShapeDtypeStruct((16, SEGMENTS, LANES), jnp.float32),
            jax.ShapeDtypeStruct((4, SEGMENTS, LANES), jnp.float32),
            jax.ShapeDtypeStruct((256, 1024), jnp.bfloat16),
        ),
        in_specs=[VMEM_SPEC] * 3,
        out_specs=(VMEM_SPEC,) * 4,
        scratch_shapes=scratch(48, 2),
        compiler_params=PARAMS,
        cost_estimate=pl.CostEstimate(flops=4 * 10**7, bytes_accessed=16 * 2**20, transcendentals=0),
        name="inner_sweeps",
    )(got, scalar, rows_matrix)


def edge_sweeps(odd, got, line_a, line_b, scalar, tile_a, tile_b, partial, kept, matrix, done, rows_matrix):
    return pl.pallas_call(
        edge_kernel,
        out_shape=jax.ShapeDtypeStruct((6 * GROUP, LANES), jnp.float32),
        in_specs=[pl.BlockSpec(memory_space=pltpu.SMEM)] + [VMEM_SPEC] * 11,
        out_specs=ANY_SPEC,
        scratch_shapes=scratch(16, 1)
        + [pltpu.VMEM((2 * GROUP, LANES), jnp.float32), pltpu.SemaphoreType.DMA((3,))],
        compiler_params=PARAMS,
        name="edge_sweeps",
    )(odd, got, line_a, line_b, scalar, tile_a, tile_b, partial, kept, matrix, done, rows_matrix)


def local(scalar, x_velocity, y_velocity):
    count = lax.axis_size("row")
    pair_a = [(i, i ^ 1) for i in range(count)]
    pair_b = [(i, (i + (1 if i % 2 else -1)) % count) for i in range(count)]
    odd = lax.axis_index("row") % 2
    tiles = scalar.reshape(6, TILE, SEGMENTS, LANES).transpose(0, 2, 1, 3).reshape(6 * GROUP, LANES)
    first, last = tiles[:GROUP], tiles[5 * GROUP :]
    tile_a = lax.ppermute(jnp.where(odd == 1, first, last), "row", pair_a)
    tile_b = lax.ppermute(jnp.where(odd == 1, last, first), "row", pair_b)
    packed = pack(x_velocity, y_velocity)
    got = lax.all_to_all(packed, "line", 0, 0, tiled=True)
    first, last = got[:, 0:2], got[:, 10:12]
    line_a = lax.ppermute(jnp.where(odd == 1, first, last), "row", pair_a)
    line_b = lax.ppermute(jnp.where(odd == 1, last, first), "row", pair_b)
    rows_matrix = rows_matrices()
    done, partial, kept, matrix = inner_sweeps(got, tiles, rows_matrix)
    result = edge_sweeps(
        odd.astype(jnp.int32).reshape(1), got, line_a, line_b, tiles, tile_a, tile_b, partial, kept, matrix, done, rows_matrix
    )
    return result.reshape(6, SEGMENTS, TILE, LANES).transpose(0, 2, 1, 3).reshape(1, 48, 3072)


def solution(mesh):
    in_specs = (P("line", "row", None), P(None, "row", "line"), P(None, "row", "line"))
    out_specs = P("line", "row", None)
    return jax.shard_map(local, mesh=mesh, in_specs=in_specs, out_specs=out_specs, check_vma=False)
```

time: 36.2 us -> 33 us (0.912)
  Pallas kernels: 9.73 us -> 7.69 us
  local copies, waits for them, and re-layouts: 2.02 us -> 0.01 us
  other arithmetic: 0 us -> 0.97 us
  waiting for transfers between devices: 6.77 us -> 5.82 us
  starting transfers between devices: 17.3 us -> 18.1 us
    pallas_call x2, Pallas kernels: 7.39 us -> 5.53 us  [the longest x1 3.9 us: inner_sweeps(): pl.pallas_call(inner_kernel, out_shape=(jax.ShapeDtypeStruct((4 * GROUP,...]
    unnamed x8 -> x4, local copies, waits for them, and re-layouts: 1.05 us -> 0.01 us
    select_n x0 -> x2, other arithmetic: none -> 0.97 us  [the longest x1 0.96 us: local(): tile_b = lax.ppermute(jnp.where(odd == 1, last, first), 'row', pair_b)]
    slice x2 -> x0, local copies, waits for them, and re-layouts: 0.97 us -> none  [the longest x1 0.96 us: local(): bottom = lax.ppermute(tiles[:GROUP], 'row', down)]
    all_to_all x1, waiting for transfers between devices: 6.76 us -> 5.81 us  [local(): got = lax.all_to_all(packed, 'line', 0, 0, tiled=True)]
    ppermute x4, starting transfers between devices: 5.71 us -> 6.56 us  [the longest x1 3.32 us: local(): line_b = lax.ppermute(jnp.where(odd == 1, last, first), 'row', pair_b)]
  transfers between devices with their start and end apart: 5 -> 5, of which waited for: 1 -> 1; matrix products, arithmetic and copies ran while one was open for 3% -> 3% of each run, Pallas kernels for 16% -> 12%
where the time goes in v3:
time: 33 us; the launch traced here: 32.7 us
  starting transfers between devices  18.1 us (55%)
  Pallas kernels  7.69 us (23%)
  waiting for transfers between devices  5.82 us (18%)
  other arithmetic  0.97 us (3%)
    all_to_all x1, starting transfers between devices, local(): got = lax.all_to_all(packed, 'line', 0, 0, tiled=True)  11.6 us
    all_to_all x1, waiting for transfers between devices, local(): got = lax.all_to_all(packed, 'line', 0, 0, tiled=True)  5.81 us
    pallas_call x1, Pallas kernels, inner_sweeps(): pl.pallas_call(inner_kernel, out_shape=(jax.ShapeDtypeStruct((4 * GROUP,...  3.9 us
    ppermute x1, starting transfers between devices, local(): line_b = lax.ppermute(jnp.where(odd == 1, last, first), 'row', pair_b)  3.32 us
    ppermute x1, starting transfers between devices, local(): tile_b = lax.ppermute(jnp.where(odd == 1, last, first), 'row', pair_b)  2.22 us
    pallas_call x1, Pallas kernels, edge_sweeps(): pl.pallas_call(edge_kernel, out_shape=jax.ShapeDtypeStruct((6 * GROUP, LA...  2.16 us
    pallas_call x1, Pallas kernels, pack(): pl.pallas_call(pack_kernel, out_shape=jax.ShapeDtypeStruct((16, 12, 128),...  1.63 us
    ppermute x1, starting transfers between devices, local(): tile_a = lax.ppermute(jnp.where(odd == 1, first, last), 'row', pair_a)  1.02 us
  transfers between devices with their start and end apart: 5, of which 1 were waited for; matrix products, arithmetic and copies ran while one was open for 3% of the time, Pallas kernels for 12%

profile of v3, /device:TPU:1, one launch (start us, length us, event | category | flops | bytes accessed | tf_op | source)
XLA Modules:
  0.0 32.7 jit_solution(2014849502189078660)
XLA Ops:
  0.0 0.0 copy-start
  0.0 1.6 %pack_planes.1 = f32[16,12,128]{2,1,0:T(8,128)} custom-call(f32[6,12,48]{2,1,0:T(8,128)} %x_ref.1, f32[6,12,48]{2,1,0:T(8,128)} %y_ref.1), custom_call_target="tpu_custom_call" | custom-call | tf_op jit(solution)/shard_map/pack_planes/pallas_call | solution.py:105
  1.6 11.6 %all-to-all-start = ((f32[16,12,128]{2,1,0:T(8,128)}), f32[16,12,128]{2,1,0:T(8,128)S(1)}, u32[]{:S(2)}, u32[]{:S(2)}) async-start(f32[16,12,128]{2,1,0:T(8,128)} %pack_planes.1), calls=%async_computation | async-start | bytes 262144 | tf_op jit(solution)/shard_map/all_to_all | solution.py:361
  13.2 1.0 %select_bitcast_fusion = (f32[192,128]{1,0:T(8,128)S(1)}, f32[192,128]{1,0:T(8,128)S(1)}) fusion(f32[6,24,8,128]{3,2,1,0:T(8,128)} %bitcast.15, pred[]{:T(512)S(6)} %eq.4), kind=kLoop, calls=%fused_computation | loop fusion | flops 49152 | bytes 393217 | tf_op jit(solution)/shard_map/jit(_where)/select_n | solution.py:359
  14.2 2.2 %collective-permute-start.3 = (f32[192,128]{1,0:T(8,128)S(1)}, f32[192,128]{1,0:T(8,128)S(1)}, u32[]{:S(2)}, u32[]{:S(2)}) collective-permute-start(f32[192,128]{1,0:T(8,128)S(1)} %get-tuple-element.13), channel_id=1, source_target_pairs={{0,240},{16,32},{32,16},{48,64},{64,48},{80,96},{96,80},{112,128},... | collective-permute-start | bytes 294920 | tf_op jit(solution)/shard_map/ppermute | solution.py:359
  16.4 1.0 %collective-permute-start.2 = (f32[192,128]{1,0:T(8,128)S(1)}, f32[192,128]{1,0:T(8,128)S(1)}, u32[]{:S(2)}, u32[]{:S(2)}) collective-permute-start(f32[192,128]{1,0:T(8,128)S(1)} %get-tuple-element.14), channel_id=1, source_target_pairs={{0,16},{16,0},{32,48},{48,32},{64,80},{80,64},{96,112},{112,96},{1... | collective-permute-start | bytes 294920 | tf_op jit(solution)/shard_map/ppermute | solution.py:358
  17.4 5.8 %all-to-all-done.got = f32[16,12,128]{2,1,0:T(8,128)S(1)} async-done(((f32[16,12,128]{2,1,0:T(8,128)}), f32[16,12,128]{2,1,0:T(8,128)S(1)}, u32[]{:S(2)}, u32[]{:S(2)}) %all-to-all-start) | async-done | bytes 98336 | tf_op jit(solution)/shard_map/all_to_all | solution.py:361
  23.3 0.0 copy-start.1
  23.3 3.3 %collective-permute-start.1 = (f32[16,2,128]{2,1,0:T(2,128)S(1)}, f32[16,2,128]{2,1,0:T(2,128)S(1)}, u32[]{:S(2)}, u32[]{:S(2)}) collective-permute-start(f32[16,2,128]{2,1,0:T(2,128)S(1)} %get-tuple-element.15), channel_id=1, source_target_pairs={{0,240},{16,32},{32,16},{48,64},{64,48},{80,96},{96,80},{112,128},... | collective-permute-start | bytes 49160 | tf_op jit(solution)/shard_map/ppermute | solution.py:364
  26.6 0.0 collective-permute-start
  26.6 0.0 copy-done
  26.6 0.0 copy-done.1
  26.6 3.9 %inner_sweeps.1 = (f32[768,128]{1,0:T(8,128)S(1)}, f32[16,24,128]{2,1,0:T(8,128)S(1)}, f32[4,24,128]{2,1,0:T(8,128)S(1)}, bf16[256,1024]{1,0:T(8,128)(2,1)S(1)}) custom-call(f32[16,12,128]{2,1,0:T(8,128)S(1)} %all-to-all-done.got, f32[1152,128]{1,0:T(8,128)S(1)} %bitcast.16, bf16[64,32]{1,0:T(8,128)(2,1)S(1)} %copy-done.1), custom_call_target="tpu_custom_call" | custom-call | flops 40000000 | bytes 16777216 | tf_op jit(solution)/shard_map/inner_sweeps/pallas_call | solution.py:321
  30.5 0.0 collective-permute-done.3.tile_b
  30.5 0.0 collective-permute-done.2.tile_a
  30.5 0.0 collective-permute-done.1.line_b
  30.5 0.0 collective-permute-done.line_a
  30.6 2.2 %edge_sweeps.1 = f32[1152,128]{1,0:T(8,128)} custom-call(s32[1]{0:T(128)} %bitcast.odd_ref, f32[16,12,128]{2,1,0:T(8,128)S(1)} %all-to-all-done.got, f32[16,2,128]{2,1,0:T(2,128)S(1)} %collective-permute-done.line_a, f32[16,2,128]{2,1,0:T(2,128)S(1)} %collective-permute-done.1.line_b, f32[1152,128]{1,0:T(8,128)S(1)} %bitcast.17, ...), custom_call_target="tpu_custom_call" | custom-call | tf_op jit(solution)/shard_map/edge_sweeps/pallas_call | solution.py:339
  (1 shorter events, 0.0 us)
Async XLA Ops:
  0.0 26.6 %copy-start = (f32[1,48,3072]{2,1,0:T(8,128)S(1)}, f32[1,48,3072]{2,1,0:T(8,128)}, u32[]{:S(2)}) copy-start(f32[1,48,3072]{2,1,0:T(8,128)} %param.4) | copy-start | bytes 1769476
  1.6 21.6 %all-to-all-start = ((f32[16,12,128]{2,1,0:T(8,128)}), f32[16,12,128]{2,1,0:T(8,128)S(1)}, u32[]{:S(2)}, u32[]{:S(2)}) async-start(f32[16,12,128]{2,1,0:T(8,128)} %pack_planes.1), calls=%async_computation | async-start | bytes 262144 | tf_op jit(solution)/shard_map/all_to_all | solution.py:361
  14.2 16.3 %collective-permute-start.3 = (f32[192,128]{1,0:T(8,128)S(1)}, f32[192,128]{1,0:T(8,128)S(1)}, u32[]{:S(2)}, u32[]{:S(2)}) collective-permute-start(f32[192,128]{1,0:T(8,128)S(1)} %get-tuple-element.13), channel_id=1, source_target_pairs={{0,240},{16,32},{32,16},{48,64},{64,48},{80,96},{96,80},{112,128},... | collective-permute-start | bytes 294920 | tf_op jit(solution)/shard_map/ppermute | solution.py:359
  16.4 14.1 %collective-permute-start.2 = (f32[192,128]{1,0:T(8,128)S(1)}, f32[192,128]{1,0:T(8,128)S(1)}, u32[]{:S(2)}, u32[]{:S(2)}) collective-permute-start(f32[192,128]{1,0:T(8,128)S(1)} %get-tuple-element.14), channel_id=1, source_target_pairs={{0,16},{16,0},{32,48},{48,32},{64,80},{80,64},{96,112},{112,96},{1... | collective-permute-start | bytes 294920 | tf_op jit(solution)/shard_map/ppermute | solution.py:358
  23.3 3.3 %copy-start.1 = (bf16[64,32]{1,0:T(8,128)(2,1)S(1)}, bf16[64,32]{1,0:T(8,128)(2,1)}, u32[]{:S(2)}) copy-start(bf16[64,32]{1,0:T(8,128)(2,1)} %constant.21.clone.rows_matrix) | copy-start | bytes 12292
  23.3 7.3 %collective-permute-start.1 = (f32[16,2,128]{2,1,0:T(2,128)S(1)}, f32[16,2,128]{2,1,0:T(2,128)S(1)}, u32[]{:S(2)}, u32[]{:S(2)}) collective-permute-start(f32[16,2,128]{2,1,0:T(2,128)S(1)} %get-tuple-element.15), channel_id=1, source_target_pairs={{0,240},{16,32},{32,16},{48,64},{64,48},{80,96},{96,80},{112,128},... | collective-permute-start | bytes 49160 | tf_op jit(solution)/shard_map/ppermute | solution.py:364
  26.6 4.0 %collective-permute-start = (f32[16,2,128]{2,1,0:T(2,128)S(1)}, f32[16,2,128]{2,1,0:T(2,128)S(1)}, u32[]{:S(2)}, u32[]{:S(2)}) collective-permute-start(f32[16,2,128]{2,1,0:T(2,128)S(1)} %get-tuple-element.16), channel_id=1, source_target_pairs={{0,16},{16,0},{32,48},{48,32},{64,80},{80,64},{96,112},{112,96},{1... | collective-permute-start | bytes 49160 | tf_op jit(solution)/shard_map/ppermute | solution.py:363

commit v4 on v3

--- a/solution.py
+++ b/solution.py
@@ -10,6 +10,7 @@
 
 SEGMENTS, LANES, TILE = 24, 128, 8
 GROUP = SEGMENTS * TILE
+PITCH = 9
 WINDOW = 64
 
 
@@ -156,13 +157,13 @@
     for q in range(4):
 
         def store(t, seg, values):
-            coefs[q, pl.ds((t * SEGMENTS + seg) * TILE, TILE), :] = values
+            coefs[q, pl.ds((t * SEGMENTS + seg) * PITCH, TILE), :] = values
 
         spread(left_x[...], matrix, slice(256 * q, 256 * q + 256), lines.shape[0], store)
 
     def store_y(t, seg, values):
-        if t < ylines.shape[0] // GROUP:
-            ylines[pl.ds((t * SEGMENTS + seg) * TILE, TILE), :] = values
+        if t < ylines.shape[0] // (SEGMENTS * PITCH):
+            ylines[pl.ds((t * SEGMENTS + seg) * PITCH, TILE), :] = values
 
     spread(left_y[...], matrix, slice(0, 256), gy.shape[0], store_y)
 
@@ -171,7 +172,12 @@
     return pl.ds((row // TILE) * GROUP + row % TILE, SEGMENTS, stride=TILE)
 
 
-def x_swept(coefs, at, value, lane):
+def field_at(row):
+    return pl.ds((row // TILE) * (SEGMENTS * PITCH) + row % TILE, SEGMENTS, stride=PITCH)
+
+
+def x_swept(coefs, row, value, lane):
+    at = field_at(row)
     v, s, dp, dm = (coefs[q, at, :] for q in range(4))
     parts = products(value, s + v * jnp.where(v >= 0.0, dp, dm))
     total, wrap = parts[4], None
@@ -186,7 +192,7 @@
 
 
 def y_products(ylines, cell, source):
-    below, here, above = (ylines[row_at(cell + k), :] for k in (-1, 0, 1))
+    below, here, above = (ylines[field_at(cell + k), :] for k in (-1, 0, 1))
     dm, dp = here - below, above - here
     for r in range(4):
         v0 = (r - 1.5) / 4
@@ -202,21 +208,30 @@
 KEPT = (2, 3, 44, 45)
 
 
-def inner_kernel(got, scalar, rows_matrix, done, partial, kept, matrix, gx, gy, left_x, left_y, coefs, ylines, moved):
+def prepare_kernel(odd_ref, scalar, fine, send_a, send_b, matrix):
+    odd = odd_ref[0] == 1
+    for y in range(48):
+        fine[y] = scalar[row_at(y), :]
+    for i in range(4):
+        first, last = fine[i], fine[44 + i]
+        send_a[i] = jnp.where(odd, first, last)
+        send_b[i] = jnp.where(odd, last, first)
+    fill_matrix(matrix)
+
+
+def inner_kernel(got, fine, matrix, rows_matrix, done, partial, kept, gx, gy, left_x, left_y, coefs, ylines, moved):
     gx[8:16, :] = jnp.zeros((8, 768), jnp.float32)
     gy[8:16, :] = jnp.zeros((8, 768), jnp.float32)
     for j in range(16):
         gx[0:12, 48 * j : 48 * j + 48] = got[j, :, 0:48]
         gy[0:12, 48 * j : 48 * j + 48] = got[j, :, 64:112]
-    fill_matrix(matrix)
     fine_fields(gx[...], gy[...], left_x, left_y, coefs, ylines, matrix, rows_matrix[0:48, :])
     lane = lanes()
 
     def x_rows(block, carry):
         for r in range(22):
             row = block * 22 + r + 2
-            at = row_at(row)
-            moved[row] = x_swept(coefs, at, scalar[at, :], lane)
+            moved[row] = x_swept(coefs, row, fine[row], lane)
         return carry
 
     lax.fori_loop(0, 2, x_rows, 0)
@@ -246,11 +261,11 @@
         partial[8 + r] = acc[r]
 
 
-def edge_kernel(odd_ref, got, line_a, line_b, scalar, tile_a, tile_b, partial, kept, matrix, done, rows_matrix, out, gx, gy, left_x, left_y, coefs, ylines, moved, edge, sems):
+def edge_kernel(odd_ref, got, line_a, line_b, fine, rows_a, rows_b, partial, kept, matrix, done, rows_matrix, out, gx, gy, left_x, left_y, coefs, ylines, moved, edge, sems):
     inner_copy = pltpu.make_async_copy(done, out.at[pl.ds(GROUP, 4 * GROUP), :], sems.at[2])
     inner_copy.start()
+    odd = odd_ref[0] == 1
     gx[8:16, :] = jnp.zeros((8, 768), jnp.float32)
-    odd = odd_ref[0] == 1
     gy[8:16, :] = jnp.zeros((8, 768), jnp.float32)
     for j in range(16):
         at = slice(48 * j, 48 * j + 48)
@@ -266,32 +281,36 @@
             moved[i] = kept[KEPT.index(y)]
             continue
         if 0 <= y < 48:
-            value = scalar[row_at(y), :]
+            value = fine[y]
         else:
-            at = row_at(y % TILE)
-            from_a, from_b = tile_a[at, :], tile_b[at, :]
+            from_a, from_b = rows_a[y % 4], rows_b[y % 4]
             value = jnp.where(odd, from_a, from_b) if y < 0 else jnp.where(odd, from_b, from_a)
-        moved[i] = x_swept(coefs, row_at(i), value, lane)
-
-    def tile_copy(side, tile):
-        return pltpu.make_async_copy(
-            edge.at[pl.ds(side * GROUP, GROUP), :], out.at[pl.ds(tile * GROUP, GROUP), :], sems.at[side]
-        )
-
-    for side, (cells, tile) in enumerate((((-1, 0), 0), ((11, 12), 5))):
-        acc = {8 * tile + r: partial[8 * side + r] for r in range(8)}
-        for k, c in enumerate(cells):
-            for r, parts in enumerate(y_products(ylines, EDGE_CELLS.index(c), lambda r: moved[8 * side + 4 * k + r])):
-                for s in range(9):
+        moved[i] = x_swept(coefs, i, value, lane)
+
+    acc = {row: partial[i] for i, row in enumerate(list(range(8)) + list(range(40, 48)))}
+    for k in range(2):
+        sides = [
+            (8 * side + 4 * k, c, y_products(ylines, EDGE_CELLS.index(c), lambda r, at=8 * side + 4 * k: moved[at + r]))
+            for side, c in ((0, k - 1), (1, k + 11))
+        ]
+        for r in range(4):
+            for at, c, values in sides:
+                for s, part in enumerate(next(values)):
                     row = 4 * c + r + s - 4
                     if row in acc:
-                        acc[row] = acc[row] + parts[s]
+                        acc[row] = acc[row] + part
+    copies = []
+    for side, tile in ((0, 0), (1, 5)):
         for r in range(8):
             edge[row_at(8 * side + r), :] = acc[8 * tile + r]
-        tile_copy(side, tile).start()
-    inner_copy.wait()
-    tile_copy(0, 0).wait()
-    tile_copy(1, 5).wait()
+        copies.append(
+            pltpu.make_async_copy(
+                edge.at[pl.ds(side * GROUP, GROUP), :], out.at[pl.ds(tile * GROUP, GROUP), :], sems.at[side]
+            )
+        )
+        copies[-1].start()
+    for copy in [inner_copy] + copies:
+        copy.wait()
 
 
 def scratch(rows, ytiles):
@@ -300,8 +319,8 @@
         pltpu.VMEM((16, 768), jnp.float32),
         pltpu.VMEM((12 * rows, 256), jnp.bfloat16),
         pltpu.VMEM((12 * 16, 256), jnp.bfloat16),
-        pltpu.VMEM((4, rows // TILE * GROUP, LANES), jnp.float32),
-        pltpu.VMEM((ytiles * GROUP, LANES), jnp.float32),
+        pltpu.VMEM((4, rows // TILE * SEGMENTS * PITCH, LANES), jnp.float32),
+        pltpu.VMEM((ytiles * SEGMENTS * PITCH, LANES), jnp.float32),
         pltpu.VMEM((rows, SEGMENTS, LANES), jnp.float32),
     ]
 
@@ -317,25 +336,41 @@
     )
 
 
-def inner_sweeps(got, scalar, rows_matrix):
+def prepare(odd, scalar):
+    rows = jax.ShapeDtypeStruct((4, SEGMENTS, LANES), jnp.float32)
+    return pl.pallas_call(
+        prepare_kernel,
+        out_shape=(
+            jax.ShapeDtypeStruct((48, SEGMENTS, LANES), jnp.float32),
+            rows,
+            rows,
+            jax.ShapeDtypeStruct((256, 1024), jnp.bfloat16),
+        ),
+        in_specs=[pl.BlockSpec(memory_space=pltpu.SMEM), VMEM_SPEC],
+        out_specs=(VMEM_SPEC,) * 4,
+        compiler_params=PARAMS,
+        name="prepare",
+    )(odd, scalar)
+
+
+def inner_sweeps(got, fine, matrix, rows_matrix):
     return pl.pallas_call(
         inner_kernel,
         out_shape=(
             jax.ShapeDtypeStruct((4 * GROUP, LANES), jnp.float32),
             jax.ShapeDtypeStruct((16, SEGMENTS, LANES), jnp.float32),
             jax.ShapeDtypeStruct((4, SEGMENTS, LANES), jnp.float32),
-            jax.ShapeDtypeStruct((256, 1024), jnp.bfloat16),
         ),
-        in_specs=[VMEM_SPEC] * 3,
-        out_specs=(VMEM_SPEC,) * 4,
+        in_specs=[VMEM_SPEC] * 4,
+        out_specs=(VMEM_SPEC,) * 3,
         scratch_shapes=scratch(48, 2),
         compiler_params=PARAMS,
         cost_estimate=pl.CostEstimate(flops=4 * 10**7, bytes_accessed=16 * 2**20, transcendentals=0),
         name="inner_sweeps",
-    )(got, scalar, rows_matrix)
-
-
-def edge_sweeps(odd, got, line_a, line_b, scalar, tile_a, tile_b, partial, kept, matrix, done, rows_matrix):
+    )(got, fine, matrix, rows_matrix)
+
+
+def edge_sweeps(odd, got, line_a, line_b, fine, rows_a, rows_b, partial, kept, matrix, done, rows_matrix):
     return pl.pallas_call(
         edge_kernel,
         out_shape=jax.ShapeDtypeStruct((6 * GROUP, LANES), jnp.float32),
@@ -345,7 +380,7 @@
         + [pltpu.VMEM((2 * GROUP, LANES), jnp.float32), pltpu.SemaphoreType.DMA((3,))],
         compiler_params=PARAMS,
         name="edge_sweeps",
-    )(odd, got, line_a, line_b, scalar, tile_a, tile_b, partial, kept, matrix, done, rows_matrix)
+    )(odd, got, line_a, line_b, fine, rows_a, rows_b, partial, kept, matrix, done, rows_matrix)
 
 
 def local(scalar, x_velocity, y_velocity):
@@ -354,18 +389,18 @@
     pair_b = [(i, (i + (1 if i % 2 else -1)) % count) for i in range(count)]
     odd = lax.axis_index("row") % 2
     tiles = scalar.reshape(6, TILE, SEGMENTS, LANES).transpose(0, 2, 1, 3).reshape(6 * GROUP, LANES)
-    first, last = tiles[:GROUP], tiles[5 * GROUP :]
-    tile_a = lax.ppermute(jnp.where(odd == 1, first, last), "row", pair_a)
-    tile_b = lax.ppermute(jnp.where(odd == 1, last, first), "row", pair_b)
-    packed = pack(x_velocity, y_velocity)
-    got = lax.all_to_all(packed, "line", 0, 0, tiled=True)
+    parity = odd.astype(jnp.int32).reshape(1)
+    got = lax.all_to_all(pack(x_velocity, y_velocity), "line", 0, 0, tiled=True)
+    fine, send_a, send_b, matrix = prepare(parity, tiles)
+    rows_a = lax.ppermute(send_a, "row", pair_a)
+    rows_b = lax.ppermute(send_b, "row", pair_b)
     first, last = got[:, 0:2], got[:, 10:12]
     line_a = lax.ppermute(jnp.where(odd == 1, first, last), "row", pair_a)
     line_b = lax.ppermute(jnp.where(odd == 1, last, first), "row", pair_b)
     rows_matrix = rows_matrices()
-    done, partial, kept, matrix = inner_sweeps(got, tiles, rows_matrix)
+    done, partial, kept = inner_sweeps(got, fine, matrix, rows_matrix)
     result = edge_sweeps(
-        odd.astype(jnp.int32).reshape(1), got, line_a, line_b, tiles, tile_a, tile_b, partial, kept, matrix, done, rows_matrix
+        parity, got, line_a, line_b, fine, rows_a, rows_b, partial, kept, matrix, done, rows_matrix
     )
     return result.reshape(6, SEGMENTS, TILE, LANES).transpose(0, 2, 1, 3).reshape(1, 48, 3072)
 

time: 33 us -> 32.7 us (level)
  local copies, waits for them, and re-layouts: 0.01 us -> 1.06 us
  other arithmetic: 0.97 us -> 0.01 us
  starting transfers between devices: 18.1 us -> 17.3 us
  waiting for transfers between devices: 5.82 us -> 6.35 us
    unnamed x4, local copies, waits for them, and re-layouts: 0.01 us -> 1.06 us
    select_n x1 -> x0, other arithmetic: 0.96 us -> none  [local(): tile_b = lax.ppermute(jnp.where(odd == 1, last, first), 'row', pair_b)]
    ppermute x2, starting transfers between devices: 3.24 us -> 2.32 us  [the longest x1 1.28 us: local(): rows_b = lax.ppermute(send_b, 'row', pair_b)]
    all_to_all x1, waiting for transfers between devices: 5.81 us -> 6.34 us  [local(): got = lax.all_to_all(pack(x_velocity, y_velocity), 'line', 0, 0, tiled=True)]
  transfers between devices with their start and end apart: 5 -> 5, of which waited for: 1 -> 1; matrix products, arithmetic and copies ran while one was open for 3% -> 0% of each run, Pallas kernels for 12% -> 12%
where the time goes in v4:
time: 32.7 us; the launch traced here: 32.4 us
  starting transfers between devices  17.3 us (53%)
  Pallas kernels  7.58 us (23%)
  waiting for transfers between devices  6.35 us (19%)
  local copies, waits for them, and re-layouts  1.06 us (3%)
    all_to_all x1, starting transfers between devices, local(): got = lax.all_to_all(pack(x_velocity, y_velocity), 'line', 0, 0, tiled=True)  11.6 us
    all_to_all x1, waiting for transfers between devices, local(): got = lax.all_to_all(pack(x_velocity, y_velocity), 'line', 0, 0, tiled=True)  6.34 us
    pallas_call x1, Pallas kernels, inner_sweeps(): pl.pallas_call(inner_kernel, out_shape=(jax.ShapeDtypeStruct((4 * GROUP,...  3.69 us
    ppermute x1, starting transfers between devices, local(): line_b = lax.ppermute(jnp.where(odd == 1, last, first), 'row', pair_b)  3.37 us
    pallas_call x1, Pallas kernels, edge_sweeps(): pl.pallas_call(edge_kernel, out_shape=jax.ShapeDtypeStruct((6 * GROUP, LA...  2.1 us
    pallas_call x1, Pallas kernels, pack(): pl.pallas_call(pack_kernel, out_shape=jax.ShapeDtypeStruct((16, 12, 128),...  1.57 us
    ppermute x1, starting transfers between devices, local(): rows_b = lax.ppermute(send_b, 'row', pair_b)  1.28 us
    unnamed x4, local copies, waits for them, and re-layouts  1.06 us
  transfers between devices with their start and end apart: 5, of which 1 were waited for; matrix products, arithmetic and copies ran while one was open for 0% of the time, Pallas kernels for 12%

profile of v4, /device:TPU:1, one launch (start us, length us, event | category | flops | bytes accessed | tf_op | source)
XLA Modules:
  0.0 32.4 jit_solution(426170040851517267)
XLA Ops:
  0.0 1.6 %pack_planes.1 = f32[16,12,128]{2,1,0:T(8,128)} custom-call(f32[6,12,48]{2,1,0:T(8,128)} %x_ref.1, f32[6,12,48]{2,1,0:T(8,128)} %y_ref.1), custom_call_target="tpu_custom_call" | custom-call | tf_op jit(solution)/shard_map/pack_planes/pallas_call | solution.py:106
  1.6 11.6 %all-to-all-start = ((f32[16,12,128]{2,1,0:T(8,128)}), f32[16,12,128]{2,1,0:T(8,128)S(1)}, u32[]{:S(2)}, u32[]{:S(2)}) async-start(f32[16,12,128]{2,1,0:T(8,128)} %pack_planes.1), calls=%async_computation | async-start | bytes 262144 | tf_op jit(solution)/shard_map/all_to_all | solution.py:393
  13.2 0.0 copy-start
  13.2 1.1 %copy-done = f32[1,48,3072]{2,1,0:T(8,128)S(1)} copy-done((f32[1,48,3072]{2,1,0:T(8,128)S(1)}, f32[1,48,3072]{2,1,0:T(8,128)}, u32[]{:S(2)}) %copy-start) | copy-done | bytes 589848
  14.2 0.2 prepare.1
  14.5 1.0 %collective-permute-start.2 = (f32[4,24,128]{2,1,0:T(8,128)S(1)}, f32[4,24,128]{2,1,0:T(8,128)S(1)}, u32[]{:S(2)}, u32[]{:S(2)}) collective-permute-start(f32[4,24,128]{2,1,0:T(8,128)S(1)} %get-tuple-element.13), channel_id=1, source_target_pairs={{0,16},{16,0},{32,48},{48,32},{64,80},{80,64},{96,112},{112,96},{1... | collective-permute-start | bytes 147464 | tf_op jit(solution)/shard_map/ppermute | solution.py:395
  15.5 1.3 %collective-permute-start.3 = (f32[4,24,128]{2,1,0:T(8,128)S(1)}, f32[4,24,128]{2,1,0:T(8,128)S(1)}, u32[]{:S(2)}, u32[]{:S(2)}) collective-permute-start(f32[4,24,128]{2,1,0:T(8,128)S(1)} %get-tuple-element.14), channel_id=1, source_target_pairs={{0,240},{16,32},{32,16},{48,64},{64,48},{80,96},{96,80},{112,128},... | collective-permute-start | bytes 147464 | tf_op jit(solution)/shard_map/ppermute | solution.py:396
  16.8 6.3 %all-to-all-done.got = f32[16,12,128]{2,1,0:T(8,128)S(1)} async-done(((f32[16,12,128]{2,1,0:T(8,128)}), f32[16,12,128]{2,1,0:T(8,128)S(1)}, u32[]{:S(2)}, u32[]{:S(2)}) %all-to-all-start) | async-done | bytes 98336 | tf_op jit(solution)/shard_map/all_to_all | solution.py:393
  23.1 0.0 copy-start.1
  23.2 3.4 %collective-permute-start.1 = (f32[16,2,128]{2,1,0:T(2,128)S(1)}, f32[16,2,128]{2,1,0:T(2,128)S(1)}, u32[]{:S(2)}, u32[]{:S(2)}) collective-permute-start(f32[16,2,128]{2,1,0:T(2,128)S(1)} %get-tuple-element.19), channel_id=1, source_target_pairs={{0,240},{16,32},{32,16},{48,64},{64,48},{80,96},{96,80},{112,128},... | collective-permute-start | bytes 49160 | tf_op jit(solution)/shard_map/ppermute | solution.py:399
  26.5 0.0 collective-permute-start
  26.5 0.0 copy-done.1
  26.5 3.7 %inner_sweeps.1 = (f32[768,128]{1,0:T(8,128)S(1)}, f32[16,24,128]{2,1,0:T(8,128)S(1)}, f32[4,24,128]{2,1,0:T(8,128)S(1)}) custom-call(f32[16,12,128]{2,1,0:T(8,128)S(1)} %all-to-all-done.got, f32[48,24,128]{2,1,0:T(8,128)S(1)} %get-tuple-element.12.fine, bf16[256,1024]{1,0:T(8,128)(2,1)S(1)} %get-tuple-element.15.matrix, bf16[64,32]{1,0:T(8,128)(2,1)S(1)} %copy-done.1), custom_call_target="tpu_custom_call" | custom-call | flops 40000000 | bytes 16777216 | tf_op jit(solution)/shard_map/inner_sweeps/pallas_call | solution.py:357
  30.2 0.0 collective-permute-done.2.rows_a
  30.2 0.0 collective-permute-done.3.rows_b
  30.2 0.0 collective-permute-done.1.line_b
  30.3 0.0 collective-permute-done.line_a
  30.3 2.1 %edge_sweeps.1 = f32[1152,128]{1,0:T(8,128)} custom-call(s32[1]{0:T(128)} %bitcast.odd_ref, f32[16,12,128]{2,1,0:T(8,128)S(1)} %all-to-all-done.got, f32[16,2,128]{2,1,0:T(2,128)S(1)} %collective-permute-done.line_a, f32[16,2,128]{2,1,0:T(2,128)S(1)} %collective-permute-done.1.line_b, f32[48,24,128]{2,1,0:T(8,128)S(1)} %get-tuple-element.12.fine, ...), custom_call_target="tpu_custom_call" | custom-call | tf_op jit(solution)/shard_map/edge_sweeps/pallas_call | solution.py:374
  (1 shorter events, 0.0 us)
Async XLA Ops:
  1.6 21.6 %all-to-all-start = ((f32[16,12,128]{2,1,0:T(8,128)}), f32[16,12,128]{2,1,0:T(8,128)S(1)}, u32[]{:S(2)}, u32[]{:S(2)}) async-start(f32[16,12,128]{2,1,0:T(8,128)} %pack_planes.1), calls=%async_computation | async-start | bytes 262144 | tf_op jit(solution)/shard_map/all_to_all | solution.py:393
  13.2 1.1 %copy-start = (f32[1,48,3072]{2,1,0:T(8,128)S(1)}, f32[1,48,3072]{2,1,0:T(8,128)}, u32[]{:S(2)}) copy-start(f32[1,48,3072]{2,1,0:T(8,128)} %param.4) | copy-start | bytes 1769476
  14.5 15.8 %collective-permute-start.2 = (f32[4,24,128]{2,1,0:T(8,128)S(1)}, f32[4,24,128]{2,1,0:T(8,128)S(1)}, u32[]{:S(2)}, u32[]{:S(2)}) collective-permute-start(f32[4,24,128]{2,1,0:T(8,128)S(1)} %get-tuple-element.13), channel_id=1, source_target_pairs={{0,16},{16,0},{32,48},{48,32},{64,80},{80,64},{96,112},{112,96},{1... | collective-permute-start | bytes 147464 | tf_op jit(solution)/shard_map/ppermute | solution.py:395
  15.5 14.7 %collective-permute-start.3 = (f32[4,24,128]{2,1,0:T(8,128)S(1)}, f32[4,24,128]{2,1,0:T(8,128)S(1)}, u32[]{:S(2)}, u32[]{:S(2)}) collective-permute-start(f32[4,24,128]{2,1,0:T(8,128)S(1)} %get-tuple-element.14), channel_id=1, source_target_pairs={{0,240},{16,32},{32,16},{48,64},{64,48},{80,96},{96,80},{112,128},... | collective-permute-start | bytes 147464 | tf_op jit(solution)/shard_map/ppermute | solution.py:396
  23.1 3.4 %copy-start.1 = (bf16[64,32]{1,0:T(8,128)(2,1)S(1)}, bf16[64,32]{1,0:T(8,128)(2,1)}, u32[]{:S(2)}) copy-start(bf16[64,32]{1,0:T(8,128)(2,1)} %constant.21.clone.rows_matrix) | copy-start | bytes 12292
  23.2 7.1 %collective-permute-start.1 = (f32[16,2,128]{2,1,0:T(2,128)S(1)}, f32[16,2,128]{2,1,0:T(2,128)S(1)}, u32[]{:S(2)}, u32[]{:S(2)}) collective-permute-start(f32[16,2,128]{2,1,0:T(2,128)S(1)} %get-tuple-element.19), channel_id=1, source_target_pairs={{0,240},{16,32},{32,16},{48,64},{64,48},{80,96},{96,80},{112,128},... | collective-permute-start | bytes 49160 | tf_op jit(solution)/shard_map/ppermute | solution.py:399
  26.5 3.7 %collective-permute-start = (f32[16,2,128]{2,1,0:T(2,128)S(1)}, f32[16,2,128]{2,1,0:T(2,128)S(1)}, u32[]{:S(2)}, u32[]{:S(2)}) collective-permute-start(f32[16,2,128]{2,1,0:T(2,128)S(1)} %get-tuple-element.20), channel_id=1, source_target_pairs={{0,16},{16,0},{32,48},{48,32},{64,80},{80,64},{96,112},{112,96},{1... | collective-permute-start | bytes 49160 | tf_op jit(solution)/shard_map/ppermute | solution.py:398

commit v5 on v4

--- a/solution.py
+++ b/solution.py
@@ -17,14 +17,16 @@
 def kernel_parts():
     a = np.polynomial.Polynomial([0.0, 1.0])
     pieces = (
-        -(a - 1) * (25 * a**4 - 38 * a**3 - 3 * a**2 + 12 * a + 12) / 12,
-        (a - 1) * (a - 2) * (25 * a**3 - 114 * a**2 + 153 * a - 48) / 24,
-        -(a - 2) * (a - 3) ** 3 * (5 * a - 8) / 24,
+        (1.5, (a - 1) * (a - 2) * (25 * a**3 - 114 * a**2 + 153 * a - 48) / 24),
+        (2.5, -(a - 2) * (a - 3) ** 3 * (5 * a - 8) / 24),
     )
     parts = []
-    for middle, piece in zip((0.5, 1.5, 2.5), pieces):
+    for middle, piece in pieces:
         coefs = piece(middle - a).coef
-        parts.append(([float(c) for c in coefs[0::2]], [float(c) for c in coefs[1::2]]))
+        for part in (coefs[0::2], coefs[1::2]):
+            quotient, rest = divmod(np.polynomial.Polynomial(part), np.polynomial.Polynomial([-0.25, 1.0]))
+            assert np.abs(rest.coef).max() < 1e-12
+            parts.append([float(c) for c in quotient.coef])
     return parts
 
 
@@ -33,31 +35,31 @@
 
 def products(value, d):
     high = d >= 0.0
-    e = d - jnp.where(high, 1.0, -1.0)
-    right = e >= 0.0
-    t = jnp.abs(e) - 0.5
+    size = jnp.abs(d)
+    right = size >= 1.0
+    t = jnp.abs(size - 1.0) - 0.5
     tau = t * t
-    vt = value * t
-    evens, odds = [None], [None]
-    for even, odd in PARTS[1:]:
-        evens.append(value * ((even[2] * tau + even[1]) * tau + even[0]))
-        odds.append(vt * ((odd[2] * tau + odd[1]) * tau + odd[0]))
-    evens[0] = 0.5 * value - (evens[1] + evens[2])
-    odds[0] = vt - (3.0 * odds[1] + 5.0 * odds[2])
-    near = [ev + od for ev, od in zip(evens, odds)]
-    far = [ev - od for ev, od in zip(evens, odds)]
-    q = {0: far[0]}
-    q[1] = jnp.where(right, near[0], far[1])
-    q[-1] = jnp.where(right, far[1], near[0])
-    q[2] = jnp.where(right, near[1], far[2])
-    q[-2] = jnp.where(right, far[2], near[1])
-    q[3] = jnp.where(right, near[2], 0.0)
-    q[-3] = jnp.where(right, 0.0, near[2])
-    out = []
-    for s in range(-4, 5):
-        up, down = q.get(s - 1), q.get(s + 1)
-        out.append(jnp.where(high, 0.0 if up is None else up, 0.0 if down is None else down))
-    return out
+    common = value * (tau - 0.25)
+    common_t = common * t
+    even1, odd1, even2, odd2 = (
+        base * (line[1] * tau + line[0]) for base, line in zip((common, common_t) * 2, PARTS)
+    )
+    even0 = 0.5 * value - (even1 + even2)
+    odd0 = value * t - (3.0 * odd1 + 5.0 * odd2)
+    far0 = even0 - odd0
+    near0 = even0 + odd0
+    near1, far1 = even1 + odd1, even1 - odd1
+    near2, far2 = even2 + odd2, even2 - odd2
+    w = {
+        1: far0,
+        2: jnp.where(right, near0, far1),
+        0: jnp.where(right, far1, near0),
+        3: jnp.where(right, near1, far2),
+        -1: jnp.where(right, far2, near1),
+        4: jnp.where(right, near2, 0.0),
+        -2: jnp.where(right, 0.0, near2),
+    }
+    return [w[0] if s == 0 else jnp.where(high, w.get(s, 0.0), w.get(-s, 0.0)) for s in range(-4, 5)]
 
 
 def fill_matrix(out):
@@ -191,14 +193,23 @@
     return (total - wrap) + moved_wrap
 
 
-def y_products(ylines, cell, source):
-    below, here, above = (ylines[field_at(cell + k), :] for k in (-1, 0, 1))
+def group_at(start, group, pitch):
+    return pl.ds(start + group * TILE * pitch, TILE, stride=pitch)
+
+
+def y_products(ylines, cell, group, source):
+    at = (group_at((k // TILE) * (SEGMENTS * PITCH) + k % TILE, group, PITCH) for k in (cell - 1, cell, cell + 1))
+    below, here, above = (ylines[rows, :] for rows in at)
     dm, dp = here - below, above - here
     for r in range(4):
         v0 = (r - 1.5) / 4
         u0 = here + v0 * (dp if v0 > 0 else dm)
         v = v0 + 0.5 * u0
         yield products(source(r), (u0 + here) + v * jnp.where(v >= 0.0, dp, dm))
+
+
+def finished(ref, row, group, values):
+    ref[group_at((row // TILE) * GROUP + row % TILE, group, TILE), :] = values
 
 
 def lanes():
@@ -238,27 +249,22 @@
     for i, row in enumerate(KEPT):
         kept[i] = moved[row]
 
-    def y_cell(cell, acc):
-        acc = acc + [None] * 4
-        for r, parts in enumerate(y_products(ylines, cell, lambda r: moved[cell * 4 + r])):
-            for s in range(9):
-                acc[r + s] = parts[s] if acc[r + s] is None else acc[r + s] + parts[s]
-        return acc
-
-    acc = [None] * 8
-    for cell in (1, 2):
-        acc = y_cell(cell, acc)
-        for r in range(4):
-            partial[4 * (cell - 1) + r] = acc[r]
-        acc = acc[4:]
-
-    for cell in range(3, 11):
-        acc = y_cell(cell, acc)
-        for r in range(4):
-            done[row_at(4 * cell - 12 + r), :] = acc[r]
-        acc = acc[4:]
-    for r in range(8):
-        partial[8 + r] = acc[r]
+    for group in range(3):
+        segs = slice(TILE * group, TILE * group + TILE)
+        acc = [None] * 8
+        for cell in range(1, 11):
+            acc = acc + [None] * 4
+            for r, parts in enumerate(y_products(ylines, cell, group, lambda r: moved[cell * 4 + r, segs, :])):
+                for s in range(9):
+                    acc[r + s] = parts[s] if acc[r + s] is None else acc[r + s] + parts[s]
+            for r in range(4):
+                if cell < 3:
+                    partial[4 * cell - 4 + r, segs, :] = acc[r]
+                else:
+                    finished(done, 4 * cell - 12 + r, group, acc[r])
+            acc = acc[4:]
+        for r in range(8):
+            partial[8 + r, segs, :] = acc[r]
 
 
 def edge_kernel(odd_ref, got, line_a, line_b, fine, rows_a, rows_b, partial, kept, matrix, done, rows_matrix, out, gx, gy, left_x, left_y, coefs, ylines, moved, edge, sems):
@@ -287,22 +293,21 @@
             value = jnp.where(odd, from_a, from_b) if y < 0 else jnp.where(odd, from_b, from_a)
         moved[i] = x_swept(coefs, i, value, lane)
 
-    acc = {row: partial[i] for i, row in enumerate(list(range(8)) + list(range(40, 48)))}
-    for k in range(2):
-        sides = [
-            (8 * side + 4 * k, c, y_products(ylines, EDGE_CELLS.index(c), lambda r, at=8 * side + 4 * k: moved[at + r]))
-            for side, c in ((0, k - 1), (1, k + 11))
-        ]
-        for r in range(4):
-            for at, c, values in sides:
-                for s, part in enumerate(next(values)):
-                    row = 4 * c + r + s - 4
-                    if row in acc:
-                        acc[row] = acc[row] + part
+    for side, first in ((0, -1), (1, 11)):
+        for group in range(3):
+            segs = slice(TILE * group, TILE * group + TILE)
+            acc = {40 * side + r: partial[8 * side + r, segs, :] for r in range(8)}
+            for k in range(2):
+                c, at = first + k, 8 * side + 4 * k
+                for r, parts in enumerate(y_products(ylines, EDGE_CELLS.index(c), group, lambda r: moved[at + r, segs, :])):
+                    for s, part in enumerate(parts):
+                        row = 4 * c + r + s - 4
+                        if row in acc:
+                            acc[row] = acc[row] + part
+            for r in range(8):
+                finished(edge, 8 * side + r, group, acc[40 * side + r])
     copies = []
     for side, tile in ((0, 0), (1, 5)):
-        for r in range(8):
-            edge[row_at(8 * side + r), :] = acc[8 * tile + r]
         copies.append(
             pltpu.make_async_copy(
                 edge.at[pl.ds(side * GROUP, GROUP), :], out.at[pl.ds(tile * GROUP, GROUP), :], sems.at[side]

time: 32.7 us -> 32.5 us (level)
  no operation moved by 1% of the time
where the time goes in v5:
time: 32.5 us; the launch traced here: 32.2 us
  starting transfers between devices  17.3 us (53%)
  Pallas kernels  7.39 us (23%)
  waiting for transfers between devices  6.35 us (20%)
  local copies, waits for them, and re-layouts  1.06 us (3%)
    all_to_all x1, starting transfers between devices, local(): got = lax.all_to_all(pack(x_velocity, y_velocity), 'line', 0, 0, tiled=True)  11.6 us
    all_to_all x1, waiting for transfers between devices, local(): got = lax.all_to_all(pack(x_velocity, y_velocity), 'line', 0, 0, tiled=True)  6.34 us
    pallas_call x1, Pallas kernels, inner_sweeps(): pl.pallas_call(inner_kernel, out_shape=(jax.ShapeDtypeStruct((4 * GROUP,...  3.49 us
    ppermute x1, starting transfers between devices, local(): line_b = lax.ppermute(jnp.where(odd == 1, last, first), 'row', pair_b)  3.37 us
    pallas_call x1, Pallas kernels, edge_sweeps(): pl.pallas_call(edge_kernel, out_shape=jax.ShapeDtypeStruct((6 * GROUP, LA...  2.1 us
    pallas_call x1, Pallas kernels, pack(): pl.pallas_call(pack_kernel, out_shape=jax.ShapeDtypeStruct((16, 12, 128),...  1.57 us
    ppermute x1, starting transfers between devices, local(): rows_b = lax.ppermute(send_b, 'row', pair_b)  1.28 us
    unnamed x4, local copies, waits for them, and re-layouts  1.06 us
  transfers between devices with their start and end apart: 5, of which 1 were waited for; matrix products, arithmetic and copies ran while one was open for 0% of the time, Pallas kernels for 12%

profile of v5, /device:TPU:1, one launch (start us, length us, event | category | flops | bytes accessed | tf_op | source)
XLA Modules:
  0.0 32.2 jit_solution(4395629968742228016)
XLA Ops:
  0.0 1.6 %pack_planes.1 = f32[16,12,128]{2,1,0:T(8,128)} custom-call(f32[6,12,48]{2,1,0:T(8,128)} %x_ref.1, f32[6,12,48]{2,1,0:T(8,128)} %y_ref.1), custom_call_target="tpu_custom_call" | custom-call | tf_op jit(solution)/shard_map/pack_planes/pallas_call | solution.py:108
  1.6 11.6 %all-to-all-start = ((f32[16,12,128]{2,1,0:T(8,128)}), f32[16,12,128]{2,1,0:T(8,128)S(1)}, u32[]{:S(2)}, u32[]{:S(2)}) async-start(f32[16,12,128]{2,1,0:T(8,128)} %pack_planes.1), calls=%async_computation | async-start | bytes 262144 | tf_op jit(solution)/shard_map/all_to_all | solution.py:398
  13.2 0.0 copy-start
  13.2 1.1 %copy-done = f32[1,48,3072]{2,1,0:T(8,128)S(1)} copy-done((f32[1,48,3072]{2,1,0:T(8,128)S(1)}, f32[1,48,3072]{2,1,0:T(8,128)}, u32[]{:S(2)}) %copy-start) | copy-done | bytes 589848
  14.2 0.2 prepare.1
  14.5 1.0 %collective-permute-start.2 = (f32[4,24,128]{2,1,0:T(8,128)S(1)}, f32[4,24,128]{2,1,0:T(8,128)S(1)}, u32[]{:S(2)}, u32[]{:S(2)}) collective-permute-start(f32[4,24,128]{2,1,0:T(8,128)S(1)} %get-tuple-element.13), channel_id=1, source_target_pairs={{0,16},{16,0},{32,48},{48,32},{64,80},{80,64},{96,112},{112,96},{1... | collective-permute-start | bytes 147464 | tf_op jit(solution)/shard_map/ppermute | solution.py:400
  15.5 1.3 %collective-permute-start.3 = (f32[4,24,128]{2,1,0:T(8,128)S(1)}, f32[4,24,128]{2,1,0:T(8,128)S(1)}, u32[]{:S(2)}, u32[]{:S(2)}) collective-permute-start(f32[4,24,128]{2,1,0:T(8,128)S(1)} %get-tuple-element.14), channel_id=1, source_target_pairs={{0,240},{16,32},{32,16},{48,64},{64,48},{80,96},{96,80},{112,128},... | collective-permute-start | bytes 147464 | tf_op jit(solution)/shard_map/ppermute | solution.py:401
  16.8 6.3 %all-to-all-done.got = f32[16,12,128]{2,1,0:T(8,128)S(1)} async-done(((f32[16,12,128]{2,1,0:T(8,128)}), f32[16,12,128]{2,1,0:T(8,128)S(1)}, u32[]{:S(2)}, u32[]{:S(2)}) %all-to-all-start) | async-done | bytes 98336 | tf_op jit(solution)/shard_map/all_to_all | solution.py:398
  23.1 0.0 copy-start.1
  23.2 3.4 %collective-permute-start.1 = (f32[16,2,128]{2,1,0:T(2,128)S(1)}, f32[16,2,128]{2,1,0:T(2,128)S(1)}, u32[]{:S(2)}, u32[]{:S(2)}) collective-permute-start(f32[16,2,128]{2,1,0:T(2,128)S(1)} %get-tuple-element.19), channel_id=1, source_target_pairs={{0,240},{16,32},{32,16},{48,64},{64,48},{80,96},{96,80},{112,128},... | collective-permute-start | bytes 49160 | tf_op jit(solution)/shard_map/ppermute | solution.py:404
  26.5 0.0 collective-permute-start
  26.5 0.0 copy-done.1
  26.5 3.5 %inner_sweeps.1 = (f32[768,128]{1,0:T(8,128)S(1)}, f32[16,24,128]{2,1,0:T(8,128)S(1)}, f32[4,24,128]{2,1,0:T(8,128)S(1)}) custom-call(f32[16,12,128]{2,1,0:T(8,128)S(1)} %all-to-all-done.got, f32[48,24,128]{2,1,0:T(8,128)S(1)} %get-tuple-element.12.fine, bf16[256,1024]{1,0:T(8,128)(2,1)S(1)} %get-tuple-element.15.matrix, bf16[64,32]{1,0:T(8,128)(2,1)S(1)} %copy-done.1), custom_call_target="tpu_custom_call" | custom-call | flops 40000000 | bytes 16777216 | tf_op jit(solution)/shard_map/inner_sweeps/pallas_call | solution.py:362
  30.0 0.0 collective-permute-done.2.rows_a
  30.0 0.0 collective-permute-done.3.rows_b
  30.1 0.0 collective-permute-done.1.line_b
  30.1 0.0 collective-permute-done.line_a
  30.1 2.1 %edge_sweeps.1 = f32[1152,128]{1,0:T(8,128)} custom-call(s32[1]{0:T(128)} %bitcast.odd_ref, f32[16,12,128]{2,1,0:T(8,128)S(1)} %all-to-all-done.got, f32[16,2,128]{2,1,0:T(2,128)S(1)} %collective-permute-done.line_a, f32[16,2,128]{2,1,0:T(2,128)S(1)} %collective-permute-done.1.line_b, f32[48,24,128]{2,1,0:T(8,128)S(1)} %get-tuple-element.12.fine, ...), custom_call_target="tpu_custom_call" | custom-call | tf_op jit(solution)/shard_map/edge_sweeps/pallas_call | solution.py:379
  (1 shorter events, 0.0 us)
Async XLA Ops:
  1.6 21.6 %all-to-all-start = ((f32[16,12,128]{2,1,0:T(8,128)}), f32[16,12,128]{2,1,0:T(8,128)S(1)}, u32[]{:S(2)}, u32[]{:S(2)}) async-start(f32[16,12,128]{2,1,0:T(8,128)} %pack_planes.1), calls=%async_computation | async-start | bytes 262144 | tf_op jit(solution)/shard_map/all_to_all | solution.py:398
  13.2 1.1 %copy-start = (f32[1,48,3072]{2,1,0:T(8,128)S(1)}, f32[1,48,3072]{2,1,0:T(8,128)}, u32[]{:S(2)}) copy-start(f32[1,48,3072]{2,1,0:T(8,128)} %param.4) | copy-start | bytes 1769476
  14.5 15.6 %collective-permute-start.2 = (f32[4,24,128]{2,1,0:T(8,128)S(1)}, f32[4,24,128]{2,1,0:T(8,128)S(1)}, u32[]{:S(2)}, u32[]{:S(2)}) collective-permute-start(f32[4,24,128]{2,1,0:T(8,128)S(1)} %get-tuple-element.13), channel_id=1, source_target_pairs={{0,16},{16,0},{32,48},{48,32},{64,80},{80,64},{96,112},{112,96},{1... | collective-permute-start | bytes 147464 | tf_op jit(solution)/shard_map/ppermute | solution.py:400
  15.5 14.5 %collective-permute-start.3 = (f32[4,24,128]{2,1,0:T(8,128)S(1)}, f32[4,24,128]{2,1,0:T(8,128)S(1)}, u32[]{:S(2)}, u32[]{:S(2)}) collective-permute-start(f32[4,24,128]{2,1,0:T(8,128)S(1)} %get-tuple-element.14), channel_id=1, source_target_pairs={{0,240},{16,32},{32,16},{48,64},{64,48},{80,96},{96,80},{112,128},... | collective-permute-start | bytes 147464 | tf_op jit(solution)/shard_map/ppermute | solution.py:401
  23.1 3.4 %copy-start.1 = (bf16[64,32]{1,0:T(8,128)(2,1)S(1)}, bf16[64,32]{1,0:T(8,128)(2,1)}, u32[]{:S(2)}) copy-start(bf16[64,32]{1,0:T(8,128)(2,1)} %constant.21.clone.rows_matrix) | copy-start | bytes 12292
  23.2 6.9 %collective-permute-start.1 = (f32[16,2,128]{2,1,0:T(2,128)S(1)}, f32[16,2,128]{2,1,0:T(2,128)S(1)}, u32[]{:S(2)}, u32[]{:S(2)}) collective-permute-start(f32[16,2,128]{2,1,0:T(2,128)S(1)} %get-tuple-element.19), channel_id=1, source_target_pairs={{0,240},{16,32},{32,16},{48,64},{64,48},{80,96},{96,80},{112,128},... | collective-permute-start | bytes 49160 | tf_op jit(solution)/shard_map/ppermute | solution.py:404
  26.5 3.5 %collective-permute-start = (f32[16,2,128]{2,1,0:T(2,128)S(1)}, f32[16,2,128]{2,1,0:T(2,128)S(1)}, u32[]{:S(2)}, u32[]{:S(2)}) collective-permute-start(f32[16,2,128]{2,1,0:T(2,128)S(1)} %get-tuple-element.20), channel_id=1, source_target_pairs={{0,16},{16,0},{32,48},{48,32},{64,80},{80,64},{96,112},{112,96},{1... | collective-permute-start | bytes 49160 | tf_op jit(solution)/shard_map/ppermute | solution.py:403

commit v6 on v5

--- a/solution.py
+++ b/solution.py
@@ -11,7 +11,7 @@
 SEGMENTS, LANES, TILE = 24, 128, 8
 GROUP = SEGMENTS * TILE
 PITCH = 9
-WINDOW = 64
+ORDER = list(range(0, 16, 2)) + list(range(1, 16, 2))
 
 
 def kernel_parts():
@@ -99,9 +99,9 @@
     both[...] = jnp.zeros_like(both)
     both[:, :, 0:48] = x_ref[...]
     both[:, :, 64:112] = y_ref[...]
-    for k in range(16):
+    for i, k in enumerate(ORDER):
         q, w = (k + 2) // 4, ((k + 2) % 4 + 0.5) / 4
-        out_ref[k] = (1 - w) * both[q] + w * both[q + 1]
+        out_ref[i] = (1 - w) * both[q] + w * both[q + 1]
 
 
 def pack(x, y):
@@ -119,27 +119,19 @@
     return high, low
 
 
-def windows(lines, left, first):
+def windows(lines, lefts, first):
     rows = lines.shape[0]
     lane0 = lax.broadcasted_iota(jnp.int32, (rows, 128), 1) == 0
+    rolled = [pltpu.roll(lines, shift, 1) for shift in (32, 96)]
     for m in range(12):
-        shift = 32 if m % 2 == 0 else 96
-        if m < 2:
-            rolled = pltpu.roll(lines, shift, 1)
-            if m == 0:
-                even = rolled
-            else:
-                odd = rolled
-        source = even if m % 2 == 0 else odd
-        at = (64 * m - 32 + shift) % 768
-        part = jnp.where(lane0, first, source[:, at : at + 128])
-        high, low = split(part)
-        left[m * rows : (m + 1) * rows, 0:128] = high
-        left[m * rows : (m + 1) * rows, 128:256] = low
-
-
-def row_start(row):
-    return (row // TILE) * GROUP + row % TILE
+        at = (64 * m - 32 + (32, 96)[m % 2]) % 768
+        high, low = split(jnp.where(lane0, first, rolled[m % 2][:, at : at + 128]))
+        row = 0
+        for left in lefts:
+            count = left.shape[0] // 12
+            for columns, part in ((slice(0, 128), high), (slice(128, 256), low)):
+                left[m * count : (m + 1) * count, columns] = part[row : row + count]
+            row += count
 
 
 def spread(left, matrix, columns, rows, store):
@@ -151,23 +143,26 @@
                 store(t, 2 * m + h, res[at : at + TILE, LANES * h : LANES * h + LANES])
 
 
-def fine_fields(gx, gy, left_x, left_y, coefs, ylines, matrix, rows_matrix):
+def x_lines(gx, rows_matrix):
     high, low = split(gx)
     lines = jnp.dot(rows_matrix[...], jnp.concatenate([high, low], axis=0), preferred_element_type=jnp.float32)
-    windows(0.8 * lines, left_x, 1.0)
-    windows(1.6 * gy, left_y, 0.0)
+    return 0.8 * lines
+
+
+def field(left, matrix, q, out):
+    def store(t, seg, values):
+        if t < out.shape[0] // (SEGMENTS * PITCH):
+            out[pl.ds((t * SEGMENTS + seg) * PITCH, TILE), :] = values
+
+    spread(left[...], matrix, slice(256 * q, 256 * q + 256), left.shape[0] // 12, store)
+
+
+def fine_fields(gx, gy, left_x, left_y, coefs, ylines, matrix, rows_matrix):
+    windows(x_lines(gx, rows_matrix), (left_x,), 1.0)
+    windows(1.6 * gy, (left_y,), 0.0)
     for q in range(4):
-
-        def store(t, seg, values):
-            coefs[q, pl.ds((t * SEGMENTS + seg) * PITCH, TILE), :] = values
-
-        spread(left_x[...], matrix, slice(256 * q, 256 * q + 256), lines.shape[0], store)
-
-    def store_y(t, seg, values):
-        if t < ylines.shape[0] // (SEGMENTS * PITCH):
-            ylines[pl.ds((t * SEGMENTS + seg) * PITCH, TILE), :] = values
-
-    spread(left_y[...], matrix, slice(0, 256), gy.shape[0], store_y)
+        field(left_x, matrix, q, coefs.at[q])
+    field(left_y, matrix, 0, ylines)
 
 
 def row_at(row):
@@ -230,19 +225,26 @@
     fill_matrix(matrix)
 
 
-def inner_kernel(got, fine, matrix, rows_matrix, done, partial, kept, gx, gy, left_x, left_y, coefs, ylines, moved):
+def inner_kernel(got, fine, matrix, rows_matrix, done, partial, kept, gx, gy, left_x, left_y, coefs, ylines, moved, left_first, coefs_first):
     gx[8:16, :] = jnp.zeros((8, 768), jnp.float32)
     gy[8:16, :] = jnp.zeros((8, 768), jnp.float32)
-    for j in range(16):
-        gx[0:12, 48 * j : 48 * j + 48] = got[j, :, 0:48]
-        gy[0:12, 48 * j : 48 * j + 48] = got[j, :, 64:112]
-    fine_fields(gx[...], gy[...], left_x, left_y, coefs, ylines, matrix, rows_matrix[0:48, :])
+    for i, j in enumerate(ORDER):
+        gx[0:12, 48 * j : 48 * j + 48] = got[i, :, 0:48]
+        gy[0:12, 48 * j : 48 * j + 48] = got[i, :, 64:112]
+    windows(x_lines(gx[...], rows_matrix[0:48, :]), (left_first, left_x), 1.0)
+    for q in range(4):
+        field(left_first, matrix, q, coefs_first.at[q])
+    windows(1.6 * gy[...], (left_y,), 0.0)
     lane = lanes()
+    for q in range(5):
+        field(left_x if q < 4 else left_y, matrix, q % 4, coefs.at[q] if q < 4 else ylines)
+        for row in range(2 + 3 * q, min(5 + 3 * q, 16)):
+            moved[row] = x_swept(coefs_first, row, fine[row], lane)
 
     def x_rows(block, carry):
-        for r in range(22):
-            row = block * 22 + r + 2
-            moved[row] = x_swept(coefs, row, fine[row], lane)
+        for r in range(15):
+            row = block * 15 + r
+            moved[row + 16] = x_swept(coefs, row, fine[row + 16], lane)
         return carry
 
     lax.fori_loop(0, 2, x_rows, 0)
@@ -273,11 +275,11 @@
     odd = odd_ref[0] == 1
     gx[8:16, :] = jnp.zeros((8, 768), jnp.float32)
     gy[8:16, :] = jnp.zeros((8, 768), jnp.float32)
-    for j in range(16):
+    for i, j in enumerate(ORDER):
         at = slice(48 * j, 48 * j + 48)
-        from_a, from_b = line_a[j], line_b[j]
+        from_a, from_b = line_a[i], line_b[i]
         below, above = jnp.where(odd, from_a, from_b), jnp.where(odd, from_b, from_a)
-        for row, values in ((0, below), (2, got[j, 0:2, :]), (4, got[j, 10:12, :]), (6, above)):
+        for row, values in ((0, below), (2, got[i, 0:2, :]), (4, got[i, 10:12, :]), (6, above)):
             gx[row : row + 2, at] = values[:, 0:48]
             gy[row : row + 2, at] = values[:, 64:112]
     fine_fields(gx[...], gy[...], left_x, left_y, coefs, ylines, matrix, rows_matrix[48:64, :])
@@ -326,7 +328,7 @@
         pltpu.VMEM((12 * 16, 256), jnp.bfloat16),
         pltpu.VMEM((4, rows // TILE * SEGMENTS * PITCH, LANES), jnp.float32),
         pltpu.VMEM((ytiles * SEGMENTS * PITCH, LANES), jnp.float32),
-        pltpu.VMEM((rows, SEGMENTS, LANES), jnp.float32),
+        pltpu.VMEM((max(rows + 16, 48) if rows > 16 else rows, SEGMENTS, LANES), jnp.float32),
     ]
 
 
@@ -368,7 +370,11 @@
         ),
         in_specs=[VMEM_SPEC] * 4,
         out_specs=(VMEM_SPEC,) * 3,
-        scratch_shapes=scratch(48, 2),
+        scratch_shapes=scratch(32, 2)
+        + [
+            pltpu.VMEM((12 * 16, 256), jnp.bfloat16),
+            pltpu.VMEM((4, 2 * SEGMENTS * PITCH, LANES), jnp.float32),
+        ],
         compiler_params=PARAMS,
         cost_estimate=pl.CostEstimate(flops=4 * 10**7, bytes_accessed=16 * 2**20, transcendentals=0),
         name="inner_sweeps",
@@ -395,7 +401,7 @@
     odd = lax.axis_index("row") % 2
     tiles = scalar.reshape(6, TILE, SEGMENTS, LANES).transpose(0, 2, 1, 3).reshape(6 * GROUP, LANES)
     parity = odd.astype(jnp.int32).reshape(1)
-    got = lax.all_to_all(pack(x_velocity, y_velocity), "line", 0, 0, tiled=True)
+    got = lax.all_to_all(pack(x_velocity, y_velocity), "line", 0, 0, axis_index_groups=[ORDER], tiled=True)
     fine, send_a, send_b, matrix = prepare(parity, tiles)
     rows_a = lax.ppermute(send_a, "row", pair_a)
     rows_b = lax.ppermute(send_b, "row", pair_b)

time: 32.5 us -> 31.3 us (0.963)
  waiting for transfers between devices: 6.35 us -> 5.31 us
    all_to_all x1, waiting for transfers between devices: 6.34 us -> 5.3 us  [local(): lax.all_to_all(pack(x_velocity, y_velocity), 'line', 0, 0, axis_index_gro...]
where the time goes in v6:
time: 31.3 us; the launch traced here: 31 us
  starting transfers between devices  17.3 us (55%)
  Pallas kernels  7.3 us (23%)
  waiting for transfers between devices  5.31 us (17%)
  local copies, waits for them, and re-layouts  1.06 us (3%)
    all_to_all x1, starting transfers between devices, local(): lax.all_to_all(pack(x_velocity, y_velocity), 'line', 0, 0, axis_index_gro...  11.6 us
    all_to_all x1, waiting for transfers between devices, local(): lax.all_to_all(pack(x_velocity, y_velocity), 'line', 0, 0, axis_index_gro...  5.3 us
    pallas_call x1, Pallas kernels, inner_sweeps(): pl.pallas_call(inner_kernel, out_shape=(jax.ShapeDtypeStruct((4 * GROUP,...  3.4 us
    ppermute x1, starting transfers between devices, local(): line_b = lax.ppermute(jnp.where(odd == 1, last, first), 'row', pair_b)  3.37 us
    pallas_call x1, Pallas kernels, edge_sweeps(): pl.pallas_call(edge_kernel, out_shape=jax.ShapeDtypeStruct((6 * GROUP, LA...  2.1 us
    pallas_call x1, Pallas kernels, pack(): pl.pallas_call(pack_kernel, out_shape=jax.ShapeDtypeStruct((16, 12, 128),...  1.57 us
    ppermute x1, starting transfers between devices, local(): rows_b = lax.ppermute(send_b, 'row', pair_b)  1.28 us
    unnamed x4, local copies, waits for them, and re-layouts  1.06 us
  transfers between devices with their start and end apart: 5, of which 1 were waited for; matrix products, arithmetic and copies ran while one was open for 0% of the time, Pallas kernels for 12%

profile of v6, /device:TPU:1, one launch (start us, length us, event | category | flops | bytes accessed | tf_op | source)
XLA Modules:
  0.0 31.0 jit_solution(5787323200184047412)
XLA Ops:
  0.0 1.6 %pack_planes.1 = f32[16,12,128]{2,1,0:T(8,128)} custom-call(f32[6,12,48]{2,1,0:T(8,128)} %x_ref.1, f32[6,12,48]{2,1,0:T(8,128)} %y_ref.1), custom_call_target="tpu_custom_call" | custom-call | tf_op jit(solution)/shard_map/pack_planes/pallas_call | solution.py:108
  1.6 11.6 %all-to-all-start = ((f32[16,12,128]{2,1,0:T(8,128)}), f32[16,12,128]{2,1,0:T(8,128)S(1)}, u32[]{:S(2)}, u32[]{:S(2)}) async-start(f32[16,12,128]{2,1,0:T(8,128)} %pack_planes.1), calls=%async_computation | async-start | bytes 262144 | tf_op jit(solution)/shard_map/all_to_all | solution.py:404
  13.2 0.0 copy-start
  13.2 1.1 %copy-done = f32[1,48,3072]{2,1,0:T(8,128)S(1)} copy-done((f32[1,48,3072]{2,1,0:T(8,128)S(1)}, f32[1,48,3072]{2,1,0:T(8,128)}, u32[]{:S(2)}) %copy-start) | copy-done | bytes 589848
  14.2 0.2 prepare.1
  14.5 1.0 %collective-permute-start.2 = (f32[4,24,128]{2,1,0:T(8,128)S(1)}, f32[4,24,128]{2,1,0:T(8,128)S(1)}, u32[]{:S(2)}, u32[]{:S(2)}) collective-permute-start(f32[4,24,128]{2,1,0:T(8,128)S(1)} %get-tuple-element.13), channel_id=1, source_target_pairs={{0,16},{16,0},{32,48},{48,32},{64,80},{80,64},{96,112},{112,96},{1... | collective-permute-start | bytes 147464 | tf_op jit(solution)/shard_map/ppermute | solution.py:406
  15.5 1.3 %collective-permute-start.3 = (f32[4,24,128]{2,1,0:T(8,128)S(1)}, f32[4,24,128]{2,1,0:T(8,128)S(1)}, u32[]{:S(2)}, u32[]{:S(2)}) collective-permute-start(f32[4,24,128]{2,1,0:T(8,128)S(1)} %get-tuple-element.14), channel_id=1, source_target_pairs={{0,240},{16,32},{32,16},{48,64},{64,48},{80,96},{96,80},{112,128},... | collective-permute-start | bytes 147464 | tf_op jit(solution)/shard_map/ppermute | solution.py:407
  16.8 5.3 %all-to-all-done.got = f32[16,12,128]{2,1,0:T(8,128)S(1)} async-done(((f32[16,12,128]{2,1,0:T(8,128)}), f32[16,12,128]{2,1,0:T(8,128)S(1)}, u32[]{:S(2)}, u32[]{:S(2)}) %all-to-all-start) | async-done | bytes 98336 | tf_op jit(solution)/shard_map/all_to_all | solution.py:404
  22.1 0.0 copy-start.1
  22.1 3.4 %collective-permute-start.1 = (f32[16,2,128]{2,1,0:T(2,128)S(1)}, f32[16,2,128]{2,1,0:T(2,128)S(1)}, u32[]{:S(2)}, u32[]{:S(2)}) collective-permute-start(f32[16,2,128]{2,1,0:T(2,128)S(1)} %get-tuple-element.19), channel_id=1, source_target_pairs={{0,240},{16,32},{32,16},{48,64},{64,48},{80,96},{96,80},{112,128},... | collective-permute-start | bytes 49160 | tf_op jit(solution)/shard_map/ppermute | solution.py:410
  25.5 0.0 collective-permute-start
  25.5 0.0 copy-done.1
  25.5 3.4 %inner_sweeps.1 = (f32[768,128]{1,0:T(8,128)S(1)}, f32[16,24,128]{2,1,0:T(8,128)S(1)}, f32[4,24,128]{2,1,0:T(8,128)S(1)}) custom-call(f32[16,12,128]{2,1,0:T(8,128)S(1)} %all-to-all-done.got, f32[48,24,128]{2,1,0:T(8,128)S(1)} %get-tuple-element.12.fine, bf16[256,1024]{1,0:T(8,128)(2,1)S(1)} %get-tuple-element.15.matrix, bf16[64,32]{1,0:T(8,128)(2,1)S(1)} %copy-done.1), custom_call_target="tpu_custom_call" | custom-call | flops 40000000 | bytes 16777216 | tf_op jit(solution)/shard_map/inner_sweeps/pallas_call | solution.py:364
  28.9 0.0 collective-permute-done.2.rows_a
  28.9 0.0 collective-permute-done.3.rows_b
  28.9 0.0 collective-permute-done.1.line_b
  28.9 0.0 collective-permute-done.line_a
  28.9 2.1 %edge_sweeps.1 = f32[1152,128]{1,0:T(8,128)} custom-call(s32[1]{0:T(128)} %bitcast.odd_ref, f32[16,12,128]{2,1,0:T(8,128)S(1)} %all-to-all-done.got, f32[16,2,128]{2,1,0:T(2,128)S(1)} %collective-permute-done.line_a, f32[16,2,128]{2,1,0:T(2,128)S(1)} %collective-permute-done.1.line_b, f32[48,24,128]{2,1,0:T(8,128)S(1)} %get-tuple-element.12.fine, ...), custom_call_target="tpu_custom_call" | custom-call | tf_op jit(solution)/shard_map/edge_sweeps/pallas_call | solution.py:385
  (1 shorter events, 0.0 us)
Async XLA Ops:
  1.6 20.5 %all-to-all-start = ((f32[16,12,128]{2,1,0:T(8,128)}), f32[16,12,128]{2,1,0:T(8,128)S(1)}, u32[]{:S(2)}, u32[]{:S(2)}) async-start(f32[16,12,128]{2,1,0:T(8,128)} %pack_planes.1), calls=%async_computation | async-start | bytes 262144 | tf_op jit(solution)/shard_map/all_to_all | solution.py:404
  13.2 1.1 %copy-start = (f32[1,48,3072]{2,1,0:T(8,128)S(1)}, f32[1,48,3072]{2,1,0:T(8,128)}, u32[]{:S(2)}) copy-start(f32[1,48,3072]{2,1,0:T(8,128)} %param.4) | copy-start | bytes 1769476
  14.5 14.4 %collective-permute-start.2 = (f32[4,24,128]{2,1,0:T(8,128)S(1)}, f32[4,24,128]{2,1,0:T(8,128)S(1)}, u32[]{:S(2)}, u32[]{:S(2)}) collective-permute-start(f32[4,24,128]{2,1,0:T(8,128)S(1)} %get-tuple-element.13), channel_id=1, source_target_pairs={{0,16},{16,0},{32,48},{48,32},{64,80},{80,64},{96,112},{112,96},{1... | collective-permute-start | bytes 147464 | tf_op jit(solution)/shard_map/ppermute | solution.py:406
  15.5 13.4 %collective-permute-start.3 = (f32[4,24,128]{2,1,0:T(8,128)S(1)}, f32[4,24,128]{2,1,0:T(8,128)S(1)}, u32[]{:S(2)}, u32[]{:S(2)}) collective-permute-start(f32[4,24,128]{2,1,0:T(8,128)S(1)} %get-tuple-element.14), channel_id=1, source_target_pairs={{0,240},{16,32},{32,16},{48,64},{64,48},{80,96},{96,80},{112,128},... | collective-permute-start | bytes 147464 | tf_op jit(solution)/shard_map/ppermute | solution.py:407
  22.1 3.4 %copy-start.1 = (bf16[64,32]{1,0:T(8,128)(2,1)S(1)}, bf16[64,32]{1,0:T(8,128)(2,1)}, u32[]{:S(2)}) copy-start(bf16[64,32]{1,0:T(8,128)(2,1)} %constant.21.clone.rows_matrix) | copy-start | bytes 12292
  22.1 6.8 %collective-permute-start.1 = (f32[16,2,128]{2,1,0:T(2,128)S(1)}, f32[16,2,128]{2,1,0:T(2,128)S(1)}, u32[]{:S(2)}, u32[]{:S(2)}) collective-permute-start(f32[16,2,128]{2,1,0:T(2,128)S(1)} %get-tuple-element.19), channel_id=1, source_target_pairs={{0,240},{16,32},{32,16},{48,64},{64,48},{80,96},{96,80},{112,128},... | collective-permute-start | bytes 49160 | tf_op jit(solution)/shard_map/ppermute | solution.py:410
  25.5 3.4 %collective-permute-start = (f32[16,2,128]{2,1,0:T(2,128)S(1)}, f32[16,2,128]{2,1,0:T(2,128)S(1)}, u32[]{:S(2)}, u32[]{:S(2)}) collective-permute-start(f32[16,2,128]{2,1,0:T(2,128)S(1)} %get-tuple-element.20), channel_id=1, source_target_pairs={{0,16},{16,0},{32,48},{48,32},{64,80},{80,64},{96,112},{112,96},{1... | collective-permute-start | bytes 49160 | tf_op jit(solution)/shard_map/ppermute | solution.py:409

commit v7 on v6

--- a/solution.py
+++ b/solution.py
@@ -11,7 +11,7 @@
 SEGMENTS, LANES, TILE = 24, 128, 8
 GROUP = SEGMENTS * TILE
 PITCH = 9
-ORDER = list(range(0, 16, 2)) + list(range(1, 16, 2))
+ORDER = [11, 15, 9, 13, 14, 10, 8, 12, 7, 5, 6, 4, 3, 1, 2, 0]
 
 
 def kernel_parts():

time: 31.3 us -> 27.7 us (0.88)
  waiting for transfers between devices: 5.31 us -> 0.59 us
  starting transfers between devices: 17.3 us -> 18.4 us
    all_to_all x1, waiting for transfers between devices: 5.3 us -> 0.58 us  [local(): lax.all_to_all(pack(x_velocity, y_velocity), 'line', 0, 0, axis_index_gro...]
    all_to_all x1, starting transfers between devices: 11.6 us -> 13.2 us  [local(): lax.all_to_all(pack(x_velocity, y_velocity), 'line', 0, 0, axis_index_gro...]
    ppermute x1, starting transfers between devices: 3.37 us -> 2.76 us  [local(): line_b = lax.ppermute(jnp.where(odd == 1, last, first), 'row', pair_b)]
  transfers between devices with their start and end apart: 5 -> 5, of which waited for: 1 -> 1; matrix products, arithmetic and copies ran while one was open for 0% -> 0% of each run, Pallas kernels for 12% -> 13%
where the time goes in v7:
time: 27.7 us; the launch traced here: 27.5 us
  starting transfers between devices  18.4 us (66%)
  Pallas kernels  7.31 us (26%)
  local copies, waits for them, and re-layouts  1.06 us (4%)
  waiting for transfers between devices  0.59 us (2%)
    all_to_all x1, starting transfers between devices, local(): lax.all_to_all(pack(x_velocity, y_velocity), 'line', 0, 0, axis_index_gro...  13.2 us
    pallas_call x1, Pallas kernels, inner_sweeps(): pl.pallas_call(inner_kernel, out_shape=(jax.ShapeDtypeStruct((4 * GROUP,...  3.4 us
    ppermute x1, starting transfers between devices, local(): line_b = lax.ppermute(jnp.where(odd == 1, last, first), 'row', pair_b)  2.76 us
    pallas_call x1, Pallas kernels, edge_sweeps(): pl.pallas_call(edge_kernel, out_shape=jax.ShapeDtypeStruct((6 * GROUP, LA...  2.11 us
    pallas_call x1, Pallas kernels, pack(): pl.pallas_call(pack_kernel, out_shape=jax.ShapeDtypeStruct((16, 12, 128),...  1.57 us
    ppermute x1, starting transfers between devices, local(): rows_b = lax.ppermute(send_b, 'row', pair_b)  1.28 us
    unnamed x4, local copies, waits for them, and re-layouts  1.06 us
    ppermute x1, starting transfers between devices, local(): rows_a = lax.ppermute(send_a, 'row', pair_a)  1.04 us
  transfers between devices with their start and end apart: 5, of which 1 were waited for; matrix products, arithmetic and copies ran while one was open for 0% of the time, Pallas kernels for 13%

profile of v7, /device:TPU:1, one launch (start us, length us, event | category | flops | bytes accessed | tf_op | source)
XLA Modules:
  0.0 27.5 jit_solution(13804925619638456413)
XLA Ops:
  0.0 1.6 %pack_planes.1 = f32[16,12,128]{2,1,0:T(8,128)} custom-call(f32[6,12,48]{2,1,0:T(8,128)} %x_ref.1, f32[6,12,48]{2,1,0:T(8,128)} %y_ref.1), custom_call_target="tpu_custom_call" | custom-call | tf_op jit(solution)/shard_map/pack_planes/pallas_call | solution.py:108
  1.6 13.2 %all-to-all-start = ((f32[16,12,128]{2,1,0:T(8,128)}), f32[16,12,128]{2,1,0:T(8,128)S(1)}, u32[]{:S(2)}, u32[]{:S(2)}) async-start(f32[16,12,128]{2,1,0:T(8,128)} %pack_planes.1), calls=%async_computation | async-start | bytes 262144 | tf_op jit(solution)/shard_map/all_to_all | solution.py:404
  14.7 0.0 copy-start
  14.7 1.1 %copy-done = f32[1,48,3072]{2,1,0:T(8,128)S(1)} copy-done((f32[1,48,3072]{2,1,0:T(8,128)S(1)}, f32[1,48,3072]{2,1,0:T(8,128)}, u32[]{:S(2)}) %copy-start) | copy-done | bytes 589848
  15.8 0.2 prepare.1
  16.0 1.0 %collective-permute-start.2 = (f32[4,24,128]{2,1,0:T(8,128)S(1)}, f32[4,24,128]{2,1,0:T(8,128)S(1)}, u32[]{:S(2)}, u32[]{:S(2)}) collective-permute-start(f32[4,24,128]{2,1,0:T(8,128)S(1)} %get-tuple-element.13), channel_id=1, source_target_pairs={{0,16},{16,0},{32,48},{48,32},{64,80},{80,64},{96,112},{112,96},{1... | collective-permute-start | bytes 147464 | tf_op jit(solution)/shard_map/ppermute | solution.py:406
  17.1 1.3 %collective-permute-start.3 = (f32[4,24,128]{2,1,0:T(8,128)S(1)}, f32[4,24,128]{2,1,0:T(8,128)S(1)}, u32[]{:S(2)}, u32[]{:S(2)}) collective-permute-start(f32[4,24,128]{2,1,0:T(8,128)S(1)} %get-tuple-element.14), channel_id=1, source_target_pairs={{0,240},{16,32},{32,16},{48,64},{64,48},{80,96},{96,80},{112,128},... | collective-permute-start | bytes 147464 | tf_op jit(solution)/shard_map/ppermute | solution.py:407
  18.3 0.6 %all-to-all-done.got = f32[16,12,128]{2,1,0:T(8,128)S(1)} async-done(((f32[16,12,128]{2,1,0:T(8,128)}), f32[16,12,128]{2,1,0:T(8,128)S(1)}, u32[]{:S(2)}, u32[]{:S(2)}) %all-to-all-start) | async-done | bytes 98336 | tf_op jit(solution)/shard_map/all_to_all | solution.py:404
  18.9 0.0 copy-start.1
  18.9 2.8 %collective-permute-start.1 = (f32[16,2,128]{2,1,0:T(2,128)S(1)}, f32[16,2,128]{2,1,0:T(2,128)S(1)}, u32[]{:S(2)}, u32[]{:S(2)}) collective-permute-start(f32[16,2,128]{2,1,0:T(2,128)S(1)} %get-tuple-element.19), channel_id=1, source_target_pairs={{0,240},{16,32},{32,16},{48,64},{64,48},{80,96},{96,80},{112,128},... | collective-permute-start | bytes 49160 | tf_op jit(solution)/shard_map/ppermute | solution.py:410
  21.7 0.2 collective-permute-start
  21.9 0.0 copy-done.1
  21.9 3.4 %inner_sweeps.1 = (f32[768,128]{1,0:T(8,128)S(1)}, f32[16,24,128]{2,1,0:T(8,128)S(1)}, f32[4,24,128]{2,1,0:T(8,128)S(1)}) custom-call(f32[16,12,128]{2,1,0:T(8,128)S(1)} %all-to-all-done.got, f32[48,24,128]{2,1,0:T(8,128)S(1)} %get-tuple-element.12.fine, bf16[256,1024]{1,0:T(8,128)(2,1)S(1)} %get-tuple-element.15.matrix, bf16[64,32]{1,0:T(8,128)(2,1)S(1)} %copy-done.1), custom_call_target="tpu_custom_call" | custom-call | flops 40000000 | bytes 16777216 | tf_op jit(solution)/shard_map/inner_sweeps/pallas_call | solution.py:364
  25.3 0.0 collective-permute-done.2.rows_a
  25.3 0.0 collective-permute-done.3.rows_b
  25.3 0.0 collective-permute-done.1.line_b
  25.3 0.0 collective-permute-done.line_a
  25.3 2.1 %edge_sweeps.1 = f32[1152,128]{1,0:T(8,128)} custom-call(s32[1]{0:T(128)} %bitcast.odd_ref, f32[16,12,128]{2,1,0:T(8,128)S(1)} %all-to-all-done.got, f32[16,2,128]{2,1,0:T(2,128)S(1)} %collective-permute-done.line_a, f32[16,2,128]{2,1,0:T(2,128)S(1)} %collective-permute-done.1.line_b, f32[48,24,128]{2,1,0:T(8,128)S(1)} %get-tuple-element.12.fine, ...), custom_call_target="tpu_custom_call" | custom-call | tf_op jit(solution)/shard_map/edge_sweeps/pallas_call | solution.py:385
  (1 shorter events, 0.0 us)
Async XLA Ops:
  1.6 17.4 %all-to-all-start = ((f32[16,12,128]{2,1,0:T(8,128)}), f32[16,12,128]{2,1,0:T(8,128)S(1)}, u32[]{:S(2)}, u32[]{:S(2)}) async-start(f32[16,12,128]{2,1,0:T(8,128)} %pack_planes.1), calls=%async_computation | async-start | bytes 262144 | tf_op jit(solution)/shard_map/all_to_all | solution.py:404
  14.7 1.1 %copy-start = (f32[1,48,3072]{2,1,0:T(8,128)S(1)}, f32[1,48,3072]{2,1,0:T(8,128)}, u32[]{:S(2)}) copy-start(f32[1,48,3072]{2,1,0:T(8,128)} %param.4) | copy-start | bytes 1769476
  16.0 9.3 %collective-permute-start.2 = (f32[4,24,128]{2,1,0:T(8,128)S(1)}, f32[4,24,128]{2,1,0:T(8,128)S(1)}, u32[]{:S(2)}, u32[]{:S(2)}) collective-permute-start(f32[4,24,128]{2,1,0:T(8,128)S(1)} %get-tuple-element.13), channel_id=1, source_target_pairs={{0,16},{16,0},{32,48},{48,32},{64,80},{80,64},{96,112},{112,96},{1... | collective-permute-start | bytes 147464 | tf_op jit(solution)/shard_map/ppermute | solution.py:406
  17.1 8.2 %collective-permute-start.3 = (f32[4,24,128]{2,1,0:T(8,128)S(1)}, f32[4,24,128]{2,1,0:T(8,128)S(1)}, u32[]{:S(2)}, u32[]{:S(2)}) collective-permute-start(f32[4,24,128]{2,1,0:T(8,128)S(1)} %get-tuple-element.14), channel_id=1, source_target_pairs={{0,240},{16,32},{32,16},{48,64},{64,48},{80,96},{96,80},{112,128},... | collective-permute-start | bytes 147464 | tf_op jit(solution)/shard_map/ppermute | solution.py:407
  18.9 3.0 %copy-start.1 = (bf16[64,32]{1,0:T(8,128)(2,1)S(1)}, bf16[64,32]{1,0:T(8,128)(2,1)}, u32[]{:S(2)}) copy-start(bf16[64,32]{1,0:T(8,128)(2,1)} %constant.21.clone.rows_matrix) | copy-start | bytes 12292
  18.9 6.4 %collective-permute-start.1 = (f32[16,2,128]{2,1,0:T(2,128)S(1)}, f32[16,2,128]{2,1,0:T(2,128)S(1)}, u32[]{:S(2)}, u32[]{:S(2)}) collective-permute-start(f32[16,2,128]{2,1,0:T(2,128)S(1)} %get-tuple-element.19), channel_id=1, source_target_pairs={{0,240},{16,32},{32,16},{48,64},{64,48},{80,96},{96,80},{112,128},... | collective-permute-start | bytes 49160 | tf_op jit(solution)/shard_map/ppermute | solution.py:410
  21.7 3.6 %collective-permute-start = (f32[16,2,128]{2,1,0:T(2,128)S(1)}, f32[16,2,128]{2,1,0:T(2,128)S(1)}, u32[]{:S(2)}, u32[]{:S(2)}) collective-permute-start(f32[16,2,128]{2,1,0:T(2,128)S(1)} %get-tuple-element.20), channel_id=1, source_target_pairs={{0,16},{16,0},{32,48},{48,32},{64,80},{80,64},{96,112},{112,96},{1... | collective-permute-start | bytes 49160 | tf_op jit(solution)/shard_map/ppermute | solution.py:409

commit v8 on v7

--- a/solution.py
+++ b/solution.py
@@ -11,7 +11,7 @@
 SEGMENTS, LANES, TILE = 24, 128, 8
 GROUP = SEGMENTS * TILE
 PITCH = 9
-ORDER = [11, 15, 9, 13, 14, 10, 8, 12, 7, 5, 6, 4, 3, 1, 2, 0]
+ORDER = [11, 15, 9, 13, 10, 14, 8, 12, 7, 5, 6, 4, 3, 1, 2, 0]
 
 
 def kernel_parts():
@@ -214,15 +214,18 @@
 KEPT = (2, 3, 44, 45)
 
 
-def prepare_kernel(odd_ref, scalar, fine, send_a, send_b, matrix):
+def prepare_kernel(odd_ref, tiles, fine, send_a, send_b, matrix, scalar, sem):
+    load = pltpu.make_async_copy(tiles, scalar, sem)
+    load.start()
+    fill_matrix(matrix)
     odd = odd_ref[0] == 1
+    load.wait()
     for y in range(48):
         fine[y] = scalar[row_at(y), :]
     for i in range(4):
         first, last = fine[i], fine[44 + i]
         send_a[i] = jnp.where(odd, first, last)
         send_b[i] = jnp.where(odd, last, first)
-    fill_matrix(matrix)
 
 
 def inner_kernel(got, fine, matrix, rows_matrix, done, partial, kept, gx, gy, left_x, left_y, coefs, ylines, moved, left_first, coefs_first):
@@ -353,8 +356,9 @@
             rows,
             jax.ShapeDtypeStruct((256, 1024), jnp.bfloat16),
         ),
-        in_specs=[pl.BlockSpec(memory_space=pltpu.SMEM), VMEM_SPEC],
+        in_specs=[pl.BlockSpec(memory_space=pltpu.SMEM), ANY_SPEC],
         out_specs=(VMEM_SPEC,) * 4,
+        scratch_shapes=[pltpu.VMEM((6 * GROUP, LANES), jnp.float32), pltpu.SemaphoreType.DMA],
         compiler_params=PARAMS,
         name="prepare",
     )(odd, scalar)

time: 27.7 us -> 27.7 us (level)
  waiting for transfers between devices: 0.59 us -> 0.23 us
    all_to_all x1, waiting for transfers between devices: 0.58 us -> 0.22 us  [local(): lax.all_to_all(pack(x_velocity, y_velocity), 'line', 0, 0, axis_index_gro...]
  transfers between devices with their start and end apart: 5 -> 5, of which waited for: 1 -> 1; matrix products, arithmetic and copies ran while one was open for 0% -> 0% of each run, Pallas kernels for 13% -> 14%
where the time goes in v8:
time: 27.7 us; the launch traced here: 27.4 us
  starting transfers between devices  18.6 us (67%)
  Pallas kernels  7.43 us (27%)
  local copies, waits for them, and re-layouts  1.06 us (4%)
    all_to_all x1, starting transfers between devices, local(): lax.all_to_all(pack(x_velocity, y_velocity), 'line', 0, 0, axis_index_gro...  13.2 us
    pallas_call x1, Pallas kernels, inner_sweeps(): pl.pallas_call(inner_kernel, out_shape=(jax.ShapeDtypeStruct((4 * GROUP,...  3.4 us
    ppermute x1, starting transfers between devices, local(): line_b = lax.ppermute(jnp.where(odd == 1, last, first), 'row', pair_b)  2.92 us
    pallas_call x1, Pallas kernels, edge_sweeps(): pl.pallas_call(edge_kernel, out_shape=jax.ShapeDtypeStruct((6 * GROUP, LA...  2.11 us
    pallas_call x1, Pallas kernels, pack(): pl.pallas_call(pack_kernel, out_shape=jax.ShapeDtypeStruct((16, 12, 128),...  1.57 us
    ppermute x1, starting transfers between devices, local(): rows_b = lax.ppermute(send_b, 'row', pair_b)  1.28 us
    unnamed x4, local copies, waits for them, and re-layouts  1.06 us
    ppermute x1, starting transfers between devices, local(): rows_a = lax.ppermute(send_a, 'row', pair_a)  1.04 us
  transfers between devices with their start and end apart: 5, of which 1 were waited for; matrix products, arithmetic and copies ran while one was open for 0% of the time, Pallas kernels for 14%

profile of v8, /device:TPU:1, one launch (start us, length us, event | category | flops | bytes accessed | tf_op | source)
XLA Modules:
  0.0 27.4 jit_solution(17662349552522925859)
XLA Ops:
  0.0 1.6 %pack_planes.1 = f32[16,12,128]{2,1,0:T(8,128)} custom-call(f32[6,12,48]{2,1,0:T(8,128)} %x_ref.1, f32[6,12,48]{2,1,0:T(8,128)} %y_ref.1), custom_call_target="tpu_custom_call" | custom-call | tf_op jit(solution)/shard_map/pack_planes/pallas_call | solution.py:108
  1.6 13.2 %all-to-all-start = ((f32[16,12,128]{2,1,0:T(8,128)}), f32[16,12,128]{2,1,0:T(8,128)S(1)}, u32[]{:S(2)}, u32[]{:S(2)}) async-start(f32[16,12,128]{2,1,0:T(8,128)} %pack_planes.1), calls=%async_computation | async-start | bytes 262144 | tf_op jit(solution)/shard_map/all_to_all | solution.py:408
  14.7 0.0 copy-start
  14.7 1.1 %copy-done = f32[1,48,3072]{2,1,0:T(8,128)S(1)} copy-done((f32[1,48,3072]{2,1,0:T(8,128)S(1)}, f32[1,48,3072]{2,1,0:T(8,128)}, u32[]{:S(2)}) %copy-start) | copy-done | bytes 589848
  15.8 0.3 %prepare.1 = (f32[48,24,128]{2,1,0:T(8,128)S(1)}, f32[4,24,128]{2,1,0:T(8,128)S(1)}, f32[4,24,128]{2,1,0:T(8,128)S(1)}, bf16[256,1024]{1,0:T(8,128)(2,1)S(1)}) custom-call(s32[1]{0:T(128)} %bitcast.odd_ref, f32[1152,128]{1,0:T(8,128)S(1)} %bitcast.11), custom_call_target="tpu_custom_call" | custom-call | tf_op jit(solution)/shard_map/prepare/pallas_call | solution.py:351
  16.1 1.0 %collective-permute-start.2 = (f32[4,24,128]{2,1,0:T(8,128)S(1)}, f32[4,24,128]{2,1,0:T(8,128)S(1)}, u32[]{:S(2)}, u32[]{:S(2)}) collective-permute-start(f32[4,24,128]{2,1,0:T(8,128)S(1)} %get-tuple-element.13), channel_id=1, source_target_pairs={{0,16},{16,0},{32,48},{48,32},{64,80},{80,64},{96,112},{112,96},{1... | collective-permute-start | bytes 147464 | tf_op jit(solution)/shard_map/ppermute | solution.py:410
  17.2 1.3 %collective-permute-start.3 = (f32[4,24,128]{2,1,0:T(8,128)S(1)}, f32[4,24,128]{2,1,0:T(8,128)S(1)}, u32[]{:S(2)}, u32[]{:S(2)}) collective-permute-start(f32[4,24,128]{2,1,0:T(8,128)S(1)} %get-tuple-element.14), channel_id=1, source_target_pairs={{0,240},{16,32},{32,16},{48,64},{64,48},{80,96},{96,80},{112,128},... | collective-permute-start | bytes 147464 | tf_op jit(solution)/shard_map/ppermute | solution.py:411
  18.5 0.2 all-to-all-done.got
  18.7 0.0 copy-start.1
  18.7 2.9 %collective-permute-start.1 = (f32[16,2,128]{2,1,0:T(2,128)S(1)}, f32[16,2,128]{2,1,0:T(2,128)S(1)}, u32[]{:S(2)}, u32[]{:S(2)}) collective-permute-start(f32[16,2,128]{2,1,0:T(2,128)S(1)} %get-tuple-element.19), channel_id=1, source_target_pairs={{0,240},{16,32},{32,16},{48,64},{64,48},{80,96},{96,80},{112,128},... | collective-permute-start | bytes 49160 | tf_op jit(solution)/shard_map/ppermute | solution.py:414
  21.6 0.2 collective-permute-start
  21.8 0.0 copy-done.1
  21.8 3.4 %inner_sweeps.1 = (f32[768,128]{1,0:T(8,128)S(1)}, f32[16,24,128]{2,1,0:T(8,128)S(1)}, f32[4,24,128]{2,1,0:T(8,128)S(1)}) custom-call(f32[16,12,128]{2,1,0:T(8,128)S(1)} %all-to-all-done.got, f32[48,24,128]{2,1,0:T(8,128)S(1)} %get-tuple-element.12.fine, bf16[256,1024]{1,0:T(8,128)(2,1)S(1)} %get-tuple-element.15.matrix, bf16[64,32]{1,0:T(8,128)(2,1)S(1)} %copy-done.1), custom_call_target="tpu_custom_call" | custom-call | flops 40000000 | bytes 16777216 | tf_op jit(solution)/shard_map/inner_sweeps/pallas_call | solution.py:368
  25.2 0.0 collective-permute-done.2.rows_a
  25.2 0.0 collective-permute-done.3.rows_b
  25.2 0.0 collective-permute-done.1.line_b
  25.2 0.0 collective-permute-done.line_a
  25.3 2.1 %edge_sweeps.1 = f32[1152,128]{1,0:T(8,128)} custom-call(s32[1]{0:T(128)} %bitcast.odd_ref, f32[16,12,128]{2,1,0:T(8,128)S(1)} %all-to-all-done.got, f32[16,2,128]{2,1,0:T(2,128)S(1)} %collective-permute-done.line_a, f32[16,2,128]{2,1,0:T(2,128)S(1)} %collective-permute-done.1.line_b, f32[48,24,128]{2,1,0:T(8,128)S(1)} %get-tuple-element.12.fine, ...), custom_call_target="tpu_custom_call" | custom-call | tf_op jit(solution)/shard_map/edge_sweeps/pallas_call | solution.py:389
  (1 shorter events, 0.0 us)
Async XLA Ops:
  1.6 17.1 %all-to-all-start = ((f32[16,12,128]{2,1,0:T(8,128)}), f32[16,12,128]{2,1,0:T(8,128)S(1)}, u32[]{:S(2)}, u32[]{:S(2)}) async-start(f32[16,12,128]{2,1,0:T(8,128)} %pack_planes.1), calls=%async_computation | async-start | bytes 262144 | tf_op jit(solution)/shard_map/all_to_all | solution.py:408
  14.7 1.1 %copy-start = (f32[1,48,3072]{2,1,0:T(8,128)S(1)}, f32[1,48,3072]{2,1,0:T(8,128)}, u32[]{:S(2)}) copy-start(f32[1,48,3072]{2,1,0:T(8,128)} %param.4) | copy-start | bytes 1769476
  16.1 9.1 %collective-permute-start.2 = (f32[4,24,128]{2,1,0:T(8,128)S(1)}, f32[4,24,128]{2,1,0:T(8,128)S(1)}, u32[]{:S(2)}, u32[]{:S(2)}) collective-permute-start(f32[4,24,128]{2,1,0:T(8,128)S(1)} %get-tuple-element.13), channel_id=1, source_target_pairs={{0,16},{16,0},{32,48},{48,32},{64,80},{80,64},{96,112},{112,96},{1... | collective-permute-start | bytes 147464 | tf_op jit(solution)/shard_map/ppermute | solution.py:410
  17.2 8.0 %collective-permute-start.3 = (f32[4,24,128]{2,1,0:T(8,128)S(1)}, f32[4,24,128]{2,1,0:T(8,128)S(1)}, u32[]{:S(2)}, u32[]{:S(2)}) collective-permute-start(f32[4,24,128]{2,1,0:T(8,128)S(1)} %get-tuple-element.14), channel_id=1, source_target_pairs={{0,240},{16,32},{32,16},{48,64},{64,48},{80,96},{96,80},{112,128},... | collective-permute-start | bytes 147464 | tf_op jit(solution)/shard_map/ppermute | solution.py:411
  18.7 3.1 %copy-start.1 = (bf16[64,32]{1,0:T(8,128)(2,1)S(1)}, bf16[64,32]{1,0:T(8,128)(2,1)}, u32[]{:S(2)}) copy-start(bf16[64,32]{1,0:T(8,128)(2,1)} %constant.21.clone.rows_matrix) | copy-start | bytes 12292
  18.7 6.5 %collective-permute-start.1 = (f32[16,2,128]{2,1,0:T(2,128)S(1)}, f32[16,2,128]{2,1,0:T(2,128)S(1)}, u32[]{:S(2)}, u32[]{:S(2)}) collective-permute-start(f32[16,2,128]{2,1,0:T(2,128)S(1)} %get-tuple-element.19), channel_id=1, source_target_pairs={{0,240},{16,32},{32,16},{48,64},{64,48},{80,96},{96,80},{112,128},... | collective-permute-start | bytes 49160 | tf_op jit(solution)/shard_map/ppermute | solution.py:414
  21.6 3.6 %collective-permute-start = (f32[16,2,128]{2,1,0:T(2,128)S(1)}, f32[16,2,128]{2,1,0:T(2,128)S(1)}, u32[]{:S(2)}, u32[]{:S(2)}) collective-permute-start(f32[16,2,128]{2,1,0:T(2,128)S(1)} %get-tuple-element.20), channel_id=1, source_target_pairs={{0,16},{16,0},{32,48},{48,32},{64,80},{80,64},{96,112},{112,96},{1... | collective-permute-start | bytes 49160 | tf_op jit(solution)/shard_map/ppermute | solution.py:413
